TPU v7x, 1024 devices: a whole 4x8x16 slice. The times are simulated.
1024 devices in a mesh: rep: 32 (over x_lo, z), fsdp: 32 (over x_hi, y, core).
Axes of the slice: x: 4 (x_hi: 2, x_lo: 2; x = x_hi * 2 + x_lo), y: 8, z: 16, core: 2. Of those that a mesh axis runs over, the one named last changes fastest.
Arguments:
- tokens: bfloat16 [196608, 4096], P(('rep', 'fsdp')), may hold values from -24 to 24
- quant_weight: bfloat16 [4096, 512], P('fsdp'), may hold values from -6 to 6
- block_scales: bfloat16 [1024], P('fsdp'), may hold values from 0.0069885254 to 0.031982422
- key_grad: bfloat16 [196608, 512], P(('rep', 'fsdp')), may hold values from -6 to 6
Outputs:
- rotated: bfloat16 [196608, 512], P(('rep', 'fsdp'))
- token_grad: bfloat16 [196608, 4096], P(('rep', 'fsdp'))
- weight_grad: bfloat16 [4096, 512], P(('rep', 'fsdp'))
All inputs are finite; a program needn't handle non-finite values.
Results may differ from a plain program's by a relative error of at most 0.023.
Values may be sent and summed in bfloat16 or wider, within the bound.
No kernel may reach another device: no remote copies, remote signals or barrier semaphores. Data moves between devices by JAX's collectives and lax.ppermute only.
A program may use at most 64 MiB of HBM per device.

v0:
```python
import math

import jax
import jax.numpy as jnp
from jax import lax
from jax.sharding import PartitionSpec as P

HEAD_DIM = 128


rope_base = 10000.0


def dequantize(quant_weight, block_scales):
    rows_per_block = quant_weight.shape[0] // block_scales.shape[0]
    scaled = quant_weight.astype(jnp.float32).reshape(
        block_scales.shape[0], rows_per_block, quant_weight.shape[1]
    )
    scaled = scaled * block_scales.astype(jnp.float32)[:, None, None]
    return scaled.reshape(quant_weight.shape).astype(jnp.bfloat16)


def rotary(projected, positions, direction):
    half_size = HEAD_DIM // 2
    steps = jnp.arange(half_size, dtype=jnp.int32).astype(jnp.float32)
    frequency = jnp.exp(steps * (-2.0 * math.log(rope_base) / HEAD_DIM))
    angles = positions[:, None] * frequency[None, :]
    cosine = jnp.cos(angles)[:, None, :]
    sine_part = direction * jnp.sin(angles)[:, None, :]
    halves = projected.reshape(projected.shape[0], -1, 2, half_size)
    leading = halves[:, :, 0]
    trailing = halves[:, :, 1]
    turned = jnp.stack(
        [leading * cosine - trailing * sine_part, trailing * cosine + leading * sine_part], axis=2
    )
    return turned.reshape(projected.shape)


def partial_rows(source, proj_grad):
    return lax.dot_general(
        source, proj_grad, (((0,), (0,)), ((), ())), preferred_element_type=jnp.float32
    )


def body(tokens, quant_weight, block_scales, key_grad):
    row_count = tokens.shape[0]
    all_codes, all_scales = (
        lax.all_gather(quant_weight, "fsdp", axis=0, tiled=True),
        lax.all_gather(block_scales, "fsdp", axis=0, tiled=True),
    )
    weight = dequantize(all_codes, all_scales)
    positions = (
        lax.axis_index("fsdp") * row_count + jnp.arange(row_count, dtype=jnp.int32)
    ).astype(jnp.float32)
    projected = jnp.dot(tokens, weight, preferred_element_type=jnp.float32)
    rotated = rotary(projected, positions, 1.0).astype(jnp.bfloat16)
    proj_grad = rotary(key_grad.astype(jnp.float32), positions, -1.0).astype(jnp.bfloat16)
    token_grad = lax.dot_general(
        proj_grad, weight, (((1,), (1,)), ((), ())), preferred_element_type=jnp.float32
    ).astype(jnp.bfloat16)
    total_rows = weight.shape[0]
    fsdp_size = lax.axis_size("fsdp")
    rep_size = lax.axis_size("rep")
    share = total_rows // (fsdp_size * rep_size)
    reordered = (
        tokens.reshape(row_count, rep_size, fsdp_size, share)
        .transpose(0, 2, 1, 3)
        .reshape(row_count, total_rows)
    )
    group_sum = lax.psum_scatter(
        partial_rows(reordered, proj_grad).astype(jnp.bfloat16),
        "fsdp",
        scatter_dimension=0,
        tiled=True,
    ).astype(jnp.float32)
    summed = lax.psum_scatter(group_sum, "rep", scatter_dimension=0, tiled=True)
    weight_grad = (summed * (1.0 / math.sqrt(row_count * fsdp_size * rep_size))).astype(
        jnp.bfloat16
    )
    return (rotated, token_grad, weight_grad)


def solution(mesh):
    return jax.shard_map(
        body,
        mesh=mesh,
        in_specs=(P(("rep", "fsdp"), None), P("fsdp", None), P("fsdp"), P(("rep", "fsdp"), None)),
        out_specs=(P(("rep", "fsdp"), None), P(("rep", "fsdp"), None), P(("rep", "fsdp"), None)),
        check_vma=False,
    )
```

profile of v0, /device:TPU:2, one launch (start us, length us, event | category | flops | bytes accessed | tf_op | source)
XLA Modules:
  0.0 334.9 jit_solution(6107711064083314986)
XLA Ops:
  7.2 0.0 reduce-scatter.5.cloned.1.call-start
  7.2 1.1 copy.15
  8.4 3.2 copy.16
  11.5 2.1 reshape.121
  13.7 2.7 copy.17
  16.3 2.6 reshape.122
  18.9 0.3 broadcast_multiply_fusion
  19.2 0.1 multiply_subtract_fusion
  19.4 4.9 %fusion = bf16[4096,512]{0,1:T(8,128)(2,1)} fusion(bf16[192,512]{0,1:T(8,128)(2,1)S(1)} %bitcast.25, bf16[192,4096]{0,1:T(8,128)(2,1)} %reshape.122), kind=kOutput, calls=%fused_computation.2 | convolution fusion | flops 807403520 | bytes 5963776 | tf_op jit(solution)/shard_map/dot_general | solution.py:40
  24.2 6.5 %copy.20 = bf16[4096,512]{1,0:T(8,128)(2,1)} copy(bf16[4096,512]{0,1:T(8,128)(2,1)} %fusion) | data formatting | bytes 8388608
  30.7 0.0 copy-start.1
  30.7 0.0 reduce-scatter.5.cloned.1.call-update
  30.7 0.0 all-gather.2.cloned.1.call-start
  30.8 0.7 all-gather.2.cloned.1.call-update
  31.5 1.3 dynamic-slice
  33.5 0.0 copy-done.1
  33.5 0.2 dynamic-update-slice
  33.7 69.5 %all-reduce = bf16[1024]{0:T(1024)(128)(2,1)S(1)} all-reduce(bf16[1024]{0:T(1024)(128)(2,1)S(1)} %dynamic-update-slice), channel_id=1, replica_groups=mesh['rep'=32,'fsdp'=32] {'fsdp'}, use_global_device_ids=true, to_apply=%add | all-reduce | flops 1024 | bytes 4096
  103.2 0.2 mul.133
  103.4 0.3 mul.134
  103.7 1.3 dynamic-slice.1
  105.6 84.1 %reduce-scatter.5.cloned.1.call-done = bf16[128,512]{1,0:T(8,128)(2,1)} async-done(((bf16[4096,512]{1,0:T(8,128)(2,1)}), bf16[128,512]{1,0:T(8,128)(2,1)}) %reduce-scatter.5.cloned.1.call-update) | async-done | bytes 131088
  189.7 1.0 copy.21
  190.8 126.5 %all-reduce.3 = f32[128,512]{0,1:T(8,128)S(1)} all-reduce(bf16[128,512]{0,1:T(8,128)(2,1)S(1)} %copy.21), channel_id=3, replica_groups=mesh['rep'=32,'fsdp'=32] {'rep'}, use_global_device_ids=true, to_apply=%region_1.0.clone | all-reduce | flops 65536 | bytes 393216
  317.3 0.1 fusion.3
  317.4 0.7 copy.19
  318.1 0.0 copy-done
  318.1 3.3 fusion.2
  321.4 0.2 copy.14
  321.7 0.1 subtract_convert_fusion
  321.8 0.8 copy.18
  322.6 5.5 %convolution_convert_fusion.1 = bf16[192,4096]{1,0:T(8,128)(2,1)} fusion(bf16[192,512]{0,1:T(8,128)(2,1)S(1)} %bitcast.26, bf16[4096,512]{1,0:T(8,128)(2,1)} %all-gather.2.cloned.1.call-done, f32[4096]{0:T(1024)S(1)} %mul.134), kind=kOutput, calls=%fused_computation.3 | convolution fusion | flops 812384256 | bytes 5980160 | tf_op jit(solution)/shard_map/dot_general | solution.py:58
  (8 shorter events, 0.1 us)
Async XLA Ops:
  7.2 182.6 %reduce-scatter.5.cloned.1.call-start = ((), (), s32[]{:S(2)}) async-start(), calls=%async_computation.2 | async-start | bytes 4325376
  30.7 2.7 copy-start.1
  30.7 287.4 %copy-start = (bf16[192,4096]{1,0:T(8,128)(2,1)S(1)}, bf16[192,4096]{1,0:T(8,128)(2,1)}, u32[]{:S(2)}) copy-start(bf16[192,4096]{1,0:T(8,128)(2,1)} %param.4) | copy-start | bytes 4718596
  30.7 287.4 %all-gather.2.cloned.1.call-start = ((), (), s32[]{:S(2)}) async-start(), calls=%async_computation.1 | async-start | bytes 4325376 | tf_op jit(solution)/shard_map/all_gather | solution.py:48
Sparse Core Ops, SparseCore 0:
  30.9 158.8 reduce-scatter.4
  195.1 102.0 all-gather.1
where the time goes:
time: 335 us
  blocking collectives  196 us (59%)
  waiting for transfers between devices  84.8 us (25%)
  local copies, waits for them, and re-layouts  24.1 us (7%)
  between operations  15.5 us (5%)
  matrix products  13.7 us (4%)
    unnamed x2, blocking collectives  196 us
    unnamed x3, waiting for transfers between devices  84.8 us
    unnamed x14, local copies, waits for them, and re-layouts  16 us
  transfers between devices with their start and end apart: 2, of which 1 were waited for; matrix products, arithmetic and copies ran while one was open for 2% of the time, Pallas kernels for 0%

commit v1 on v0

v1 whole, which is shorter than its diff:
```python
import math

import jax
import jax.numpy as jnp
from jax import lax
from jax.experimental import pallas as pl
from jax.experimental.pallas import tpu as pltpu
from jax.sharding import Mesh
from jax.sharding import PartitionSpec as P

HEAD_DIM = 128
HALF = HEAD_DIM // 2
rope_base = 10000.0

SIZES = {"xl": 2, "zh": 8, "zl": 2, "xh": 2, "yh": 4, "yl": 2, "c": 2}
REP = ("xl", "zh", "zl")
FSDP = ("xh", "yh", "yl", "c")
NEAR = ("xl", "zl", "xh", "yl")
FAR = ("zh", "yh")
SWAP = [(0, 1), (1, 0)]


def dequantize(quant_weight, block_scales):
    rows_per_block = quant_weight.shape[0] // block_scales.shape[0]
    scaled = quant_weight.astype(jnp.float32).reshape(
        block_scales.shape[0], rows_per_block, quant_weight.shape[1]
    )
    scaled = scaled * block_scales.astype(jnp.float32)[:, None, None]
    return scaled.reshape(quant_weight.shape).astype(jnp.bfloat16)


def tables(positions):
    steps = jnp.arange(HALF, dtype=jnp.int32).astype(jnp.float32)
    frequency = jnp.exp(steps * (-2.0 * math.log(rope_base) / HEAD_DIM))
    angles = positions.astype(jnp.float32)[:, None] * frequency[None, :]
    cosine, sine = jnp.cos(angles), jnp.sin(angles)
    return jnp.concatenate([cosine, cosine], 1), jnp.concatenate([-sine, sine], 1)


def turn(values, cosine, sine, heads):
    parts = []
    for h in range(heads):
        part = values[:, h * HEAD_DIM : (h + 1) * HEAD_DIM]
        parts.append(part * cosine + pltpu.roll(part, HALF, 1) * sine)
    return parts


def grad_kernel(own, other, kg_own, kg_other, cos, sin, pick, out, proj_grad):
    rows = own.shape[0]
    heads = kg_own.shape[1] // HEAD_DIM

    @pl.when(pl.program_id(0) == 0)
    def _():
        for k, source in enumerate((kg_own, kg_other)):
            at = pl.ds(k * rows, rows)
            parts = turn(source[...].astype(jnp.float32), cos[at, :], -sin[at, :], heads)
            for h, part in enumerate(parts):
                proj_grad[at, h * HEAD_DIM : (h + 1) * HEAD_DIM] = part.astype(jnp.bfloat16)

    wide = pick.shape[1]
    for b in range(own.shape[1] // wide):
        at = slice(b * wide, (b + 1) * wide)
        chunk = jnp.concatenate([own[:, at], other[:, at]], 0)
        picked = lax.dot_general(
            pick[...], chunk, (((1,), (1,)), ((), ())), preferred_element_type=jnp.float32
        ).astype(jnp.bfloat16)
        partial = jnp.dot(picked, proj_grad[...], preferred_element_type=jnp.float32)
        partial = partial.astype(jnp.bfloat16)
        for k in range(8):
            out[0, k, b] = partial[k * 16 : (k + 1) * 16]


def weight_partial(own, other, kg_own, kg_other, cos, sin, pick):
    rows, features = own.shape
    kvw = kg_own.shape[1]
    blocks = 4
    width = features // 4
    whole = lambda a: pl.BlockSpec(a.shape, lambda s: (0, 0))
    return pl.pallas_call(
        grad_kernel,
        grid=(4,),
        out_shape=jax.ShapeDtypeStruct((2, 8, 8, 16, kvw), jnp.bfloat16),
        in_specs=[
            pl.BlockSpec((rows, width), lambda s: (0, s)),
            pl.BlockSpec((rows, width), lambda s: (0, s)),
            whole(kg_own),
            whole(kg_other),
            whole(cos),
            whole(sin),
            whole(pick),
        ],
        out_specs=pl.BlockSpec((1, 8, blocks, 16, kvw), lambda s: (s // 2, 0, s % 2, 0, 0)),
        scratch_shapes=[pltpu.VMEM((2 * rows, kvw), jnp.bfloat16)],
        compiler_params=pltpu.CompilerParams(vmem_limit_bytes=32 * 2**20),
        cost_estimate=pl.CostEstimate(
            flops=6 * rows * features * kvw // 2, bytes_accessed=6 * 2**20, transcendentals=0
        ),
        name="weight_partial",
    )(own, other, kg_own, kg_other, cos, sin, pick)


def forward_kernel(core, tokens, key_grad, cos, sin, w_own, w_other, rotated, token_grad, weight, sems):
    heads = key_grad.shape[1] // HEAD_DIM
    c = core[0]
    copies = []
    for y in range(8):
        pair = [
            pltpu.make_async_copy(w_own.at[y], weight.at[:, y, c], sems.at[0, y]),
            pltpu.make_async_copy(w_other.at[y], weight.at[:, y, 1 - c], sems.at[1, y]),
        ]
        for copy in pair:
            copy.start()
        copies.append(pair)
    cosine, sine = cos[...], sin[...]
    parts = turn(key_grad[...].astype(jnp.float32), cosine, -sine, heads)
    proj_grad = jnp.concatenate([p.astype(jnp.bfloat16) for p in parts], 1)
    projected = jnp.zeros(key_grad.shape, jnp.float32)
    for y in range(8):
        for copy in copies[y]:
            copy.wait()
        for xh in range(2):
            at = slice((xh * 8 + y) * 256, (xh * 8 + y + 1) * 256)
            block = weight[xh, y].reshape(256, key_grad.shape[1])
            projected = projected + jnp.dot(
                tokens[:, at], block, preferred_element_type=jnp.float32
            )
            token_grad[:, at] = lax.dot_general(
                proj_grad, block, (((1,), (1,)), ((), ())), preferred_element_type=jnp.float32
            ).astype(jnp.bfloat16)
    for h, part in enumerate(turn(projected, cosine, sine, heads)):
        rotated[:, h * HEAD_DIM : (h + 1) * HEAD_DIM] = part.astype(jnp.bfloat16)


def forward(core, tokens, key_grad, cos, sin, w_own, w_other):
    rows, features = tokens.shape
    kvw = key_grad.shape[1]
    vmem = pl.BlockSpec(memory_space=pltpu.VMEM)
    return pl.pallas_call(
        forward_kernel,
        out_shape=(
            jax.ShapeDtypeStruct((rows, kvw), jnp.bfloat16),
            jax.ShapeDtypeStruct((rows, features), jnp.bfloat16),
        ),
        in_specs=[pl.BlockSpec(memory_space=pltpu.SMEM)]
        + [vmem] * 4
        + [pl.BlockSpec(memory_space=pl.ANY)] * 2,
        out_specs=(vmem, vmem),
        scratch_shapes=[
            pltpu.VMEM((2, 8, 2, 128, kvw), jnp.bfloat16),
            pltpu.SemaphoreType.DMA((2, 8)),
        ],
        compiler_params=pltpu.CompilerParams(vmem_limit_bytes=32 * 2**20),
        cost_estimate=pl.CostEstimate(
            flops=4 * rows * features * kvw, bytes_accessed=8 * 2**20, transcendentals=0
        ),
        name="forward",
    )(core, tokens, key_grad, cos, sin, w_own, w_other)


def pick_matrix(core):
    q = lax.broadcasted_iota(jnp.int32, (128, 256), 0)
    lane = lax.broadcasted_iota(jnp.int32, (128, 256), 1)
    zl_xh, yl, yh, j = q // 32, q // 16 % 2, q // 4 % 4, q % 4
    return (lane == zl_xh * 64 + yh * 16 + yl * 8 + core * 4 + j).astype(jnp.bfloat16)


def body(tokens, quant_weight, block_scales, key_grad):
    rows = tokens.shape[0]
    kvw = key_grad.shape[1]
    core = lax.axis_index("c")
    xh = lax.axis_index("xh")
    place = lax.axis_index(FSDP)

    other_tokens = lax.ppermute(tokens, "c", SWAP)
    other_key_grad = lax.ppermute(key_grad, "c", SWAP)

    shard = dequantize(quant_weight, block_scales)
    across = lax.ppermute(shard, ("xl", "xh"), [(i, 3 - i) for i in range(4)])
    both = jnp.where(xh == 0, jnp.stack([shard, across]), jnp.stack([across, shard]))
    w_own = lax.all_gather(both, ("yh", "yl"), axis=0)

    offsets = jnp.arange(rows, dtype=jnp.int32)
    positions = jnp.concatenate([place * rows + offsets, (place + 1 - 2 * core) * rows + offsets])
    cos, sin = tables(positions)

    partial = weight_partial(
        tokens, other_tokens, key_grad, other_key_grad, cos, sin, pick_matrix(core)
    )
    near = lax.all_to_all(partial.reshape(16, 128, kvw), NEAR, 0, 0)
    near_sum = near.astype(jnp.float32).sum(0).astype(jnp.bfloat16)
    far = lax.all_to_all(near_sum.reshape(32, 4, kvw), FAR, 0, 0)
    summed = far.astype(jnp.float32).sum(0)
    count = rows * math.prod(SIZES.values())
    weight_grad = (summed * (1.0 / math.sqrt(count))).astype(jnp.bfloat16)

    w_other = lax.ppermute(w_own, "c", SWAP)
    rotated, token_grad = forward(
        core.reshape(1), tokens, key_grad, cos[:rows], sin[:rows], w_own, w_other
    )
    return (rotated, token_grad, weight_grad)


def solution(mesh):
    fine = Mesh(mesh.devices.reshape(tuple(SIZES.values())), tuple(SIZES))
    everywhere = P(REP + FSDP, None)
    return jax.shard_map(
        body,
        mesh=fine,
        in_specs=(everywhere, P(FSDP, None), P(FSDP), everywhere),
        out_specs=(everywhere, everywhere, everywhere),
        check_vma=False,
    )
```

time: 335 us -> 157 us (0.47)
  blocking collectives: 196 us -> 0 us
  starting transfers between devices: 0.08 us -> 43.3 us
  local copies, waits for them, and re-layouts: 24.1 us -> 3.41 us
  matrix products: 13.7 us -> 0 us
  Pallas kernels: 0 us -> 12 us
  waiting for transfers between devices: 84.8 us -> 78.6 us
  other arithmetic: 0.73 us -> 5.02 us
    unnamed x2 -> x0, blocking collectives: 196 us -> none
    unnamed x3 -> x1, waiting for transfers between devices: 84.8 us -> 0.02 us
    all_gather x1, waiting for transfers between devices: 0.01 us -> 45.9 us  [body(): w_own = lax.all_gather(both, ('yh', 'yl'), axis=0)]
    all_to_all x0 -> x2, starting transfers between devices: none -> 33.6 us  [the longest x1 17.5 us: body(): near = lax.all_to_all(partial.reshape(16, 128, kvw), NEAR, 0, 0)]
    ppermute x0 -> x4, waiting for transfers between devices: none -> 22 us  [the longest x1 22 us: body(): across = lax.ppermute(shard, ('xl', 'xh'), [(i, 3 - i) for i in range(4)])]
    dot_general x3 -> x0, matrix products: 13.7 us -> none  [the longest x1 5.47 us: body(): lax.dot_general(proj_grad, weight, (((1,), (1,)), ((), ())), preferred_el...]
    unnamed x14 -> x20, local copies, waits for them, and re-layouts: 16 us -> 2.54 us
    pallas_call x0 -> x2, Pallas kernels: none -> 12 us  [the longest x1 6.03 us: forward(): pl.pallas_call(forward_kernel, out_shape=(jax.ShapeDtypeStruct((rows, kvw...]
  transfers between devices with their start and end apart: 2 -> 7, of which waited for: 1 -> 3; matrix products, arithmetic and copies ran while one was open for 2% -> 3% of each run, Pallas kernels for 0% -> 4%
where the time goes in v1:
time: 157 us
  waiting for transfers between devices  78.6 us (50%)
  starting transfers between devices  43.3 us (28%)
  between operations  14.4 us (9%)
  Pallas kernels  12 us (8%)
  other arithmetic  5.02 us (3%)
  local copies, waits for them, and re-layouts  3.41 us (2%)
    all_gather x1, waiting for transfers between devices, body(): w_own = lax.all_gather(both, ('yh', 'yl'), axis=0)  45.9 us
    ppermute x1, waiting for transfers between devices, body(): across = lax.ppermute(shard, ('xl', 'xh'), [(i, 3 - i) for i in range(4)])  22 us
    all_to_all x1, starting transfers between devices, body(): near = lax.all_to_all(partial.reshape(16, 128, kvw), NEAR, 0, 0)  17.5 us
    all_to_all x1, starting transfers between devices, body(): far = lax.all_to_all(near_sum.reshape(32, 4, kvw), FAR, 0, 0)  16.1 us
    all_to_all x1, waiting for transfers between devices, body(): far = lax.all_to_all(near_sum.reshape(32, 4, kvw), FAR, 0, 0)  10.7 us
    pallas_call x1, Pallas kernels, forward(): pl.pallas_call(forward_kernel, out_shape=(jax.ShapeDtypeStruct((rows, kvw...  6.03 us
    pallas_call x1, Pallas kernels, weight_partial(): pl.pallas_call(grad_kernel, grid=(4,), out_shape=jax.ShapeDtypeStruct((2,...  5.92 us
    ppermute x1, starting transfers between devices, body(): across = lax.ppermute(shard, ('xl', 'xh'), [(i, 3 - i) for i in range(4)])  3.33 us
  transfers between devices with their start and end apart: 7, of which 3 were waited for; matrix products, arithmetic and copies ran while one was open for 3% of the time, Pallas kernels for 4%

profile of v1, /device:TPU:2, one launch (start us, length us, event | category | flops | bytes accessed | tf_op | source)
XLA Modules:
  0.0 156.7 jit_solution(2724444924883507968)
XLA Ops:
  7.2 2.1 %collective-permute-start.2 = (bf16[192,4096]{1,0:T(8,128)(2,1)}, bf16[192,4096]{1,0:T(8,128)(2,1)S(1)}, u32[]{:S(2)}, u32[]{:S(2)}) collective-permute-start(bf16[192,4096]{1,0:T(8,128)(2,1)} %own.1), channel_id=1, source_target_pairs={{0,1},{1,0},{2,3},{3,2},{4,5},{5,4},{6,7},{7,6},{8,9},{9,8},{10,11... | collective-permute-start | bytes 4718600 | tf_op jit(solution)/shard_map/ppermute | solution.py:174
  9.2 2.4 %collective-permute-start.3 = (bf16[192,512]{1,0:T(8,128)(2,1)}, bf16[192,512]{1,0:T(8,128)(2,1)S(1)}, u32[]{:S(2)}, u32[]{:S(2)}) collective-permute-start(bf16[192,512]{1,0:T(8,128)(2,1)} %kg_own.1), channel_id=1, source_target_pairs={{0,1},{1,0},{2,3},{3,2},{4,5},{5,4},{6,7},{7,6},{8,9},{9,8},{10,11... | collective-permute-start | bytes 589832 | tf_op jit(solution)/shard_map/ppermute | solution.py:175
  11.8 0.1 add_convert_fusion
  11.8 0.8 multiply_sine_fusion
  12.6 0.0 copy-start.6
  12.6 0.1 pad_maximum_fusion.cos
  12.8 0.1 pad_maximum_fusion.1.sin
  12.9 0.3 fusion.9.pick
  13.2 0.9 copy-done.2
  14.1 5.9 %weight_partial.1 = bf16[2,8,8,16,512]{4,3,2,1,0:T(8,128)(2,1)} custom-call(bf16[192,4096]{1,0:T(8,128)(2,1)S(1)} %copy-done, bf16[192,4096]{1,0:T(8,128)(2,1)S(1)} %collective-permute-done.2.other, bf16[192,512]{1,0:T(8,128)(2,1)S(1)} %copy-done.2, bf16[192,512]{1,0:T(8,128)(2,1)S(1)} %collective-permute-done.3.kg_other, ...), custom_call_target="tpu_custom_call" | custom-call | flops 1207959552 | bytes 6291456 | tf_op jit(solution)/shard_map/weight_partial/pallas_call | solution.py:79
  20.1 17.5 %all-to-all-start = ((bf16[16,128,512]{2,1,0:T(8,128)(2,1)}), bf16[16,128,512]{2,1,0:T(8,128)(2,1)}, u32[]{:S(2)}, u32[]{:S(2)}) async-start(bf16[16,128,512]{2,1,0:T(8,128)(2,1)} %bitcast.3), calls=%async_computation | async-start | bytes 4194304 | tf_op jit(solution)/shard_map/all_to_all | solution.py:189
  37.6 0.0 copy-start.7
  37.6 0.0 all-gather.2.cloned.1.call-start
  37.7 0.1 mul.92
  37.7 0.1 mul.93
  37.9 0.1 multiply_convert_fusion
  37.9 3.3 %collective-permute-start = (bf16[128,512]{1,0:T(8,128)(2,1)S(1)}, bf16[128,512]{1,0:T(8,128)(2,1)S(1)}, u32[]{:S(2)}, u32[]{:S(2)}) collective-permute-start(bf16[128,512]{1,0:T(8,128)(2,1)S(1)} %multiply_convert_fusion), channel_id=1, source_target_pairs={{0,528},{16,512},{512,16},{528,0},{1,529},{17,513},{513,17},{529,1... | collective-permute-start | bytes 393224 | tf_op jit(solution)/shard_map/ppermute | solution.py:178
  41.3 0.1 fusion.14
  41.4 22.0 %collective-permute-done = bf16[128,512]{1,0:T(8,128)(2,1)S(1)} collective-permute-done((bf16[128,512]{1,0:T(8,128)(2,1)S(1)}, bf16[128,512]{1,0:T(8,128)(2,1)S(1)}, u32[]{:S(2)}, u32[]{:S(2)}) %collective-permute-start) | collective-permute-done | bytes 131104 | tf_op jit(solution)/shard_map/ppermute | solution.py:178
  63.4 0.7 maximum_select_fusion
  64.1 0.0 all-gather.2.cloned.1.call-update
  64.1 45.9 %all-gather.2.cloned.1.call-done.w_own = bf16[8,2,128,512]{3,2,1,0:T(8,128)(2,1)} async-done(((bf16[1,2,128,512]{3,2,1,0:T(8,128)(2,1)}), bf16[8,2,128,512]{3,2,1,0:T(8,128)(2,1)}) %all-gather.2.cloned.1.call-update) | async-done | bytes 2097168 | tf_op jit(solution)/shard_map/all_gather | solution.py:180
  110.0 1.9 %collective-permute-start.1 = (bf16[8,2,128,512]{3,2,1,0:T(8,128)(2,1)}, bf16[8,2,128,512]{3,2,1,0:T(8,128)(2,1)}, u32[]{:S(2)}, u32[]{:S(2)}) collective-permute-start(bf16[8,2,128,512]{3,2,1,0:T(8,128)(2,1)} %all-gather.2.cloned.1.call-done.w_own), channel_id=1, source_target_pairs={{0,1},{1,0},{2,3},{3,2},{4,5},{5,4},{6,7},{7,6},{8,9},{9,8},{10,11... | collective-permute-start | bytes 6291464 | tf_op jit(solution)/shard_map/ppermute | solution.py:196
  111.9 1.9 %reduce_sum.21 = bf16[128,512]{1,0:T(8,128)(2,1)S(1)} reduce(bf16[16,128,512]{2,1,0:T(8,128)(2,1)} %all-to-all-done, bf16[]{:T(256)} %constant.102.clone.1), dimensions={0}, to_apply=%region_0.1 | reduce | flops 983040 | bytes 2228226 | tf_op jit(solution)/shard_map/reduce_sum | solution.py:190
  113.8 0.7 reshape.99
  114.5 16.1 %all-to-all-start.1 = ((bf16[32,4,512]{2,1,0:T(4,128)(2,1)}), bf16[32,4,512]{2,1,0:T(4,128)(2,1)S(1)}, u32[]{:S(2)}, u32[]{:S(2)}) async-start(bf16[32,4,512]{2,1,0:T(4,128)(2,1)} %reshape.99), calls=%async_computation.1 | async-start | bytes 262144 | tf_op jit(solution)/shard_map/all_to_all | solution.py:191
  130.6 0.1 fusion.10.sin
  130.7 0.1 fusion.11.cos
  130.9 1.6 %copy-done.1 = bf16[8,2,128,512]{3,2,1,0:T(8,128)(2,1)S(1)} copy-done((bf16[8,2,128,512]{3,2,1,0:T(8,128)(2,1)S(1)}, bf16[8,2,128,512]{3,2,1,0:T(8,128)(2,1)}, u32[]{:S(2)}) %copy-start.1) | copy-done | bytes 2097176
  132.4 6.0 %forward.1 = (bf16[192,512]{1,0:T(8,128)(2,1)}, bf16[192,4096]{1,0:T(8,128)(2,1)}) custom-call(s32[1]{0:T(128)} %bitcast.core, bf16[192,4096]{1,0:T(8,128)(2,1)S(1)} %copy-done, bf16[192,512]{1,0:T(8,128)(2,1)S(1)} %copy-done.3, f32[192,128]{1,0:T(8,128)S(1)} %fusion.11.cos, f32[192,128]{1,0:T(8,128)S(1)} %fusion.10.sin, ...), custom_call_target="tpu_custom_call" | custom-call | flops 1610612736 | bytes 8388608 | tf_op jit(solution)/shard_map/forward/pallas_call | solution.py:138
  138.5 10.7 %all-to-all-done.1 = bf16[32,4,512]{2,1,0:T(4,128)(2,1)S(1)} async-done(((bf16[32,4,512]{2,1,0:T(4,128)(2,1)}), bf16[32,4,512]{2,1,0:T(4,128)(2,1)S(1)}, u32[]{:S(2)}, u32[]{:S(2)}) %all-to-all-start.1) | async-done | bytes 131104 | tf_op jit(solution)/shard_map/all_to_all | solution.py:191
  149.3 0.6 multiply_convert_fusion.1
  (29 shorter events, 0.1 us)
Async XLA Ops:
  7.2 6.0 %copy-start = (bf16[192,4096]{1,0:T(8,128)(2,1)S(1)}, bf16[192,4096]{1,0:T(8,128)(2,1)}, u32[]{:S(2)}) copy-start(bf16[192,4096]{1,0:T(8,128)(2,1)} %own.1) | copy-start | bytes 4718596
  7.2 6.0 %collective-permute-start.2 = (bf16[192,4096]{1,0:T(8,128)(2,1)}, bf16[192,4096]{1,0:T(8,128)(2,1)S(1)}, u32[]{:S(2)}, u32[]{:S(2)}) collective-permute-start(bf16[192,4096]{1,0:T(8,128)(2,1)} %own.1), channel_id=1, source_target_pairs={{0,1},{1,0},{2,3},{3,2},{4,5},{5,4},{6,7},{7,6},{8,9},{9,8},{10,11... | collective-permute-start | bytes 4718600 | tf_op jit(solution)/shard_map/ppermute | solution.py:174
  9.2 3.9 %collective-permute-start.3 = (bf16[192,512]{1,0:T(8,128)(2,1)}, bf16[192,512]{1,0:T(8,128)(2,1)S(1)}, u32[]{:S(2)}, u32[]{:S(2)}) collective-permute-start(bf16[192,512]{1,0:T(8,128)(2,1)} %kg_own.1), channel_id=1, source_target_pairs={{0,1},{1,0},{2,3},{3,2},{4,5},{5,4},{6,7},{7,6},{8,9},{9,8},{10,11... | collective-permute-start | bytes 589832 | tf_op jit(solution)/shard_map/ppermute | solution.py:175
  12.6 7.4 %copy-start.4 = (f32[384,64]{1,0:T(8,128)}, f32[384,64]{1,0:T(8,128)S(1)}, u32[]{:S(2)}) copy-start(f32[384,64]{1,0:T(8,128)S(1)} %get-tuple-element.7) | copy-start | bytes 294916
  12.6 7.4 %copy-start.6 = (f32[384,64]{1,0:T(8,128)}, f32[384,64]{1,0:T(8,128)S(1)}, u32[]{:S(2)}) copy-start(f32[384,64]{1,0:T(8,128)S(1)} %get-tuple-element.8) | copy-start | bytes 294916
  13.2 0.9 copy-start.2
  20.1 17.6 %copy-start.9 = (bf16[32]{0:T(256)(128)(2,1)S(1)}, bf16[32]{0:T(256)(128)(2,1)}, u32[]{:S(2)}) copy-start(bf16[32]{0:T(256)(128)(2,1)} %param.6) | copy-start | bytes 196
  20.1 17.8 %copy-start.8 = (bf16[128,512]{1,0:T(8,128)(2,1)S(1)}, bf16[128,512]{1,0:T(8,128)(2,1)}, u32[]{:S(2)}) copy-start(bf16[128,512]{1,0:T(8,128)(2,1)} %param.5) | copy-start | bytes 393220
  20.1 91.8 %all-to-all-start = ((bf16[16,128,512]{2,1,0:T(8,128)(2,1)}), bf16[16,128,512]{2,1,0:T(8,128)(2,1)}, u32[]{:S(2)}, u32[]{:S(2)}) async-start(bf16[16,128,512]{2,1,0:T(8,128)(2,1)} %bitcast.3), calls=%async_computation | async-start | bytes 4194304 | tf_op jit(solution)/shard_map/all_to_all | solution.py:189
  37.6 93.0 %copy-start.5 = (f32[384,64]{1,0:T(8,128)S(1)}, f32[384,64]{1,0:T(8,128)}, u32[]{:S(2)}) copy-start(f32[384,64]{1,0:T(8,128)} %copy-done.4) | copy-start | bytes 294916
  37.6 93.0 %copy-start.7 = (f32[384,64]{1,0:T(8,128)S(1)}, f32[384,64]{1,0:T(8,128)}, u32[]{:S(2)}) copy-start(f32[384,64]{1,0:T(8,128)} %copy-done.6) | copy-start | bytes 294916
  37.6 72.4 %all-gather.2.cloned.1.call-start = ((), (), s32[]{:S(2)}) async-start(), calls=%async_computation.2 | async-start | bytes 2359296 | tf_op jit(solution)/shard_map/all_gather | solution.py:180
  37.9 25.4 %collective-permute-start = (bf16[128,512]{1,0:T(8,128)(2,1)S(1)}, bf16[128,512]{1,0:T(8,128)(2,1)S(1)}, u32[]{:S(2)}, u32[]{:S(2)}) collective-permute-start(bf16[128,512]{1,0:T(8,128)(2,1)S(1)} %multiply_convert_fusion), channel_id=1, source_target_pairs={{0,528},{16,512},{512,16},{528,0},{1,529},{17,513},{513,17},{529,1... | collective-permute-start | bytes 393224 | tf_op jit(solution)/shard_map/ppermute | solution.py:178
  63.4 67.5 %copy-start.3 = (bf16[192,512]{1,0:T(8,128)(2,1)S(1)}, bf16[192,512]{1,0:T(8,128)(2,1)}, u32[]{:S(2)}) copy-start(bf16[192,512]{1,0:T(8,128)(2,1)} %kg_own.1) | copy-start | bytes 589828
  110.0 20.8 %collective-permute-start.1 = (bf16[8,2,128,512]{3,2,1,0:T(8,128)(2,1)}, bf16[8,2,128,512]{3,2,1,0:T(8,128)(2,1)}, u32[]{:S(2)}, u32[]{:S(2)}) collective-permute-start(bf16[8,2,128,512]{3,2,1,0:T(8,128)(2,1)} %all-gather.2.cloned.1.call-done.w_own), channel_id=1, source_target_pairs={{0,1},{1,0},{2,3},{3,2},{4,5},{5,4},{6,7},{7,6},{8,9},{9,8},{10,11... | collective-permute-start | bytes 6291464 | tf_op jit(solution)/shard_map/ppermute | solution.py:196
  114.5 34.7 %all-to-all-start.1 = ((bf16[32,4,512]{2,1,0:T(4,128)(2,1)}), bf16[32,4,512]{2,1,0:T(4,128)(2,1)S(1)}, u32[]{:S(2)}, u32[]{:S(2)}) async-start(bf16[32,4,512]{2,1,0:T(4,128)(2,1)} %reshape.99), calls=%async_computation.1 | async-start | bytes 262144 | tf_op jit(solution)/shard_map/all_to_all | solution.py:191
  130.8 1.6 %copy-start.1 = (bf16[8,2,128,512]{3,2,1,0:T(8,128)(2,1)S(1)}, bf16[8,2,128,512]{3,2,1,0:T(8,128)(2,1)}, u32[]{:S(2)}) copy-start(bf16[8,2,128,512]{3,2,1,0:T(8,128)(2,1)} %all-gather.2.cloned.1.call-done.w_own) | copy-start | bytes 6291460
Sparse Core Ops, SparseCore 0:
  64.2 45.7 all-gather.1

commit v2 on v0

v2 whole, which is shorter than its diff:
```python
import math

import jax
import jax.numpy as jnp
from jax import lax
from jax.experimental import pallas as pl
from jax.experimental.pallas import tpu as pltpu
from jax.sharding import Mesh
from jax.sharding import PartitionSpec as P

HEAD_DIM = 128
HALF = HEAD_DIM // 2
rope_base = 10000.0

SIZES = {"xl": 2, "zh": 8, "zl": 2, "xh": 2, "yh": 4, "yl": 2, "c": 2}
REP = ("xl", "zh", "zl")
FSDP = ("xh", "yh", "yl", "c")
NEAR = ("xl", "zl", "xh", "c")
FAR = ("zh", "yh", "yl")
SWAP = [(0, 1), (1, 0)]
GRANT = 32 * 2**20
QUICK = pl.CostEstimate(flops=0, bytes_accessed=0, transcendentals=0)


def dequantize_kernel(scales, quant, out):
    rows, groups = quant.shape[0], scales.shape[1]
    group = lax.broadcasted_iota(jnp.int32, (rows, groups), 0) // (rows // groups)
    lane = lax.broadcasted_iota(jnp.int32, (rows, groups), 1)
    spread = jnp.where(group == lane, scales[...].astype(jnp.float32), 0.0)
    scale = jnp.sum(spread, axis=1, keepdims=True)
    out[...] = (quant[...].astype(jnp.float32) * scale).astype(jnp.bfloat16)


def dequantize(quant_weight, block_scales):
    return pl.pallas_call(
        dequantize_kernel,
        out_shape=jax.ShapeDtypeStruct(quant_weight.shape, jnp.bfloat16),
        name="dequantize",
    )(block_scales.reshape(1, -1), quant_weight)


def pair_kernel(xh, own, across, out):
    out[xh[0]] = own[...]
    out[1 - xh[0]] = across[...]


def pair(xh, own, across):
    vmem = pl.BlockSpec(memory_space=pltpu.VMEM)
    return pl.pallas_call(
        pair_kernel,
        out_shape=jax.ShapeDtypeStruct((2,) + own.shape, own.dtype),
        in_specs=[pl.BlockSpec(memory_space=pltpu.SMEM), vmem, vmem],
        out_specs=vmem,
        name="pair",
    )(xh.reshape(1), own, across)


def gather(across_xh):
    right = [(i, (i + 1) % 8) for i in range(8)]
    left = [(i, (i + 7) % 8) for i in range(8)]
    axes = ("yh", "yl")
    rights, lefts = [across_xh], [across_xh]
    for _ in range(3):
        rights.append(lax.ppermute(rights[-1], axes, right))
        lefts.append(lax.ppermute(lefts[-1], axes, left))
    rights.append(lax.ppermute(rights[-1], axes, right))
    return rights + lefts[1:]


def near_kernel(near, after_right, after_left, out):
    chips, cores, rows, width = near.shape
    for r in range(0, rows, 16):
        at = slice(r, r + 16)
        for c in range(cores):
            total = near[0, c, at].astype(jnp.float32)
            for chip in range(1, chips):
                total = total + near[chip, c, at].astype(jnp.float32)
            out[at, c * width : (c + 1) * width] = total.astype(jnp.bfloat16)


def near_total(near, after_right, after_left):
    chips, cores, rows, width = near.shape
    vmem = pl.BlockSpec(memory_space=pltpu.VMEM)
    anywhere = pl.BlockSpec(memory_space=pl.ANY)
    return pl.pallas_call(
        near_kernel,
        out_shape=jax.ShapeDtypeStruct((rows, cores * width), jnp.bfloat16),
        in_specs=[vmem, anywhere, anywhere],
        out_specs=vmem,
        compiler_params=pltpu.CompilerParams(vmem_limit_bytes=GRANT),
        cost_estimate=QUICK,
        name="near_total",
    )(near, after_right, after_left)


def tables(positions):
    lane = jnp.arange(HEAD_DIM, dtype=jnp.int32)
    steps = (lane % HALF).astype(jnp.float32)
    frequency = jnp.exp(steps * (-2.0 * math.log(rope_base) / HEAD_DIM))
    angles = positions.astype(jnp.float32)[:, None] * frequency[None, :]
    sign = jnp.where(lane < HALF, -1.0, 1.0)[None, :]
    return jnp.cos(angles), sign * jnp.sin(angles)


def turn(values, cosine, sine, heads):
    parts = []
    for h in range(heads):
        part = values[:, h * HEAD_DIM : (h + 1) * HEAD_DIM]
        parts.append(part * cosine + pltpu.roll(part, HALF, 1) * sine)
    return parts


def grad_kernel(core, own, other, kg_own, kg_other, cos, sin, after, out, proj_grad):
    rows, features = own.shape
    width = proj_grad.shape[1]
    mine = pl.multiple_of(core[0] * width, width)
    for k, source in enumerate((kg_own, kg_other)):
        at = pl.ds(k * rows, rows)
        values = source[:, pl.ds(mine, width)].astype(jnp.float32)
        parts = turn(values, cos[at, :], -sin[at, :], width // HEAD_DIM)
        for h, part in enumerate(parts):
            proj_grad[at, h * HEAD_DIM : (h + 1) * HEAD_DIM] = part.astype(jnp.bfloat16)

    low = lax.broadcasted_iota(jnp.int32, (8, width), 0) < 4
    for block in range(features // 256):
        at = slice(block * 256, (block + 1) * 256)
        partial = lax.dot_general(
            jnp.concatenate([own[:, at], other[:, at]], 0),
            proj_grad[...],
            (((0,), (0,)), ((), ())),
            preferred_element_type=jnp.float32,
        )
        xl, zh = divmod(block, 8)
        for k in range(4):
            first, second = [], []
            for y in range(0, 8, 2):
                start = k * 64 + y * 8
                even, odd = partial[start : start + 8], partial[start + 8 : start + 16]
                first.append(jnp.where(low, even, pltpu.roll(odd, 4, 0)))
                second.append(jnp.where(low, pltpu.roll(even, 4, 0), odd))
            out[xl, k, 0, zh] = jnp.concatenate(first, 0).astype(jnp.bfloat16)
            out[xl, k, 1, zh] = jnp.concatenate(second, 0).astype(jnp.bfloat16)


def weight_partial(core, own, other, kg_own, kg_other, cos, sin, after):
    rows, features = own.shape
    kvw = kg_own.shape[1]
    vmem = pl.BlockSpec(memory_space=pltpu.VMEM)
    return pl.pallas_call(
        grad_kernel,
        out_shape=jax.ShapeDtypeStruct((2, 4, 2, 8, 32, kvw // 2), jnp.bfloat16),
        in_specs=[pl.BlockSpec(memory_space=pltpu.SMEM)]
        + [vmem] * 6
        + [pl.BlockSpec(memory_space=pl.ANY)],
        out_specs=vmem,
        scratch_shapes=[pltpu.VMEM((2 * rows, kvw // 2), jnp.bfloat16)],
        compiler_params=pltpu.CompilerParams(vmem_limit_bytes=GRANT),
        cost_estimate=QUICK,
        name="weight_partial",
    )(core, own, other, kg_own, kg_other, cos, sin, after)


def forward_kernel(
    place, own, other, kg_own, kg_other, cos, sin, *refs
):
    blocks, (after, p_own, p_other, t_own, t_other, proj_grad, total) = refs[:8], refs[8:]
    rows, kvw = kg_own.shape
    core, y = place[0], place[1]
    for k, source in enumerate((kg_own, kg_other)):
        at = pl.ds(k * rows, rows)
        parts = turn(source[...].astype(jnp.float32), cos[at, :], -sin[at, :], kvw // HEAD_DIM)
        for h, part in enumerate(parts):
            proj_grad[at, h * HEAD_DIM : (h + 1) * HEAD_DIM] = part.astype(jnp.bfloat16)
    for k, block in enumerate(blocks):
        there = lax.rem(y + (8 - k if k <= 4 else k - 4), 8)
        weight = block[...].reshape(256, kvw)
        taken = []
        for source in (own, other):
            halves = [
                source[:, pl.ds(pl.multiple_of((xh * 8 + there) * 256 + core * 128, 128), 128)]
                for xh in range(2)
            ]
            taken.append(jnp.concatenate(halves, 1))
        share = jnp.dot(jnp.concatenate(taken, 0), weight, preferred_element_type=jnp.float32)
        total[...] = share if k == 0 else total[...] + share
        back = lax.dot_general(
            proj_grad[...], weight, (((1,), (1,)), ((), ())), preferred_element_type=jnp.float32
        ).astype(jnp.bfloat16)
        for xh in range(2):
            at = pl.ds(pl.multiple_of((xh * 8 + there) * 128, 128), 128)
            t_own[:, at] = back[:rows, xh * 128 : (xh + 1) * 128]
            t_other[:, at] = back[rows:, xh * 128 : (xh + 1) * 128]
    p_own[...] = total[:rows]
    p_other[...] = total[rows:]


def forward(place, own, other, kg_own, kg_other, cos, sin, blocks, after):
    rows, features = own.shape
    kvw = kg_own.shape[1]
    vmem = pl.BlockSpec(memory_space=pltpu.VMEM)
    return pl.pallas_call(
        forward_kernel,
        out_shape=[jax.ShapeDtypeStruct((rows, kvw), jnp.float32)] * 2
        + [jax.ShapeDtypeStruct((rows, features // 2), jnp.bfloat16)] * 2,
        in_specs=[pl.BlockSpec(memory_space=pltpu.SMEM)]
        + [vmem] * 14
        + [pl.BlockSpec(memory_space=pl.ANY)],
        out_specs=[vmem] * 4,
        scratch_shapes=[
            pltpu.VMEM((2 * rows, kvw), jnp.bfloat16),
            pltpu.VMEM((2 * rows, kvw), jnp.float32),
        ],
        compiler_params=pltpu.CompilerParams(vmem_limit_bytes=GRANT),
        cost_estimate=QUICK,
        name="forward",
    )(place, own, other, kg_own, kg_other, cos, sin, *blocks, after)


def finish_kernel(core, p_own, p_other, t_own, t_other, cos, sin, rotated, token_grad):
    kvw = p_own.shape[1]
    total = p_own[...] + p_other[...]
    for h, part in enumerate(turn(total, cos[...], sin[...], kvw // HEAD_DIM)):
        rotated[:, h * HEAD_DIM : (h + 1) * HEAD_DIM] = part.astype(jnp.bfloat16)
    for f in range(t_own.shape[1] // 128):
        at = slice(f * 128, (f + 1) * 128)
        for source, parity in ((t_own, core[0]), (t_other, 1 - core[0])):
            column = pl.multiple_of(f * 256 + parity * 128, 128)
            token_grad[:, pl.ds(column, 128)] = source[:, at]


def finish(core, p_own, p_other, t_own, t_other, cos, sin):
    rows, kvw = p_own.shape
    features = 2 * t_own.shape[1]
    steps = 3
    block = lambda width: pl.BlockSpec((rows // steps, width), lambda s: (s, 0))
    return pl.pallas_call(
        finish_kernel,
        grid=(steps,),
        out_shape=(
            jax.ShapeDtypeStruct((rows, kvw), jnp.bfloat16),
            jax.ShapeDtypeStruct((rows, features), jnp.bfloat16),
        ),
        in_specs=[pl.BlockSpec(memory_space=pltpu.SMEM)]
        + [block(kvw)] * 2
        + [block(features // 2)] * 2
        + [block(HEAD_DIM)] * 2,
        out_specs=(block(kvw), block(features)),
        compiler_params=pltpu.CompilerParams(vmem_limit_bytes=GRANT),
        cost_estimate=QUICK,
        name="finish",
    )(core, p_own, p_other, t_own, t_other, cos, sin)


def body(tokens, quant_weight, block_scales, key_grad):
    rows = tokens.shape[0]
    kvw = key_grad.shape[1]
    core = lax.axis_index("c")
    xh = lax.axis_index("xh")
    place = lax.axis_index(FSDP)

    shard = dequantize(quant_weight, block_scales)
    across = lax.ppermute(shard, ("xl", "xh"), [(i, 3 - i) for i in range(4)])
    both = pair(xh, shard, across)
    blocks = gather(both)

    other_tokens = lax.ppermute(tokens, "c", SWAP)
    other_key_grad = lax.ppermute(key_grad, "c", SWAP)

    offsets = jnp.arange(rows, dtype=jnp.int32)
    positions = jnp.concatenate([place * rows + offsets, (place + 1 - 2 * core) * rows + offsets])
    cos, sin = tables(positions)

    partial = weight_partial(
        core.reshape(1), tokens, other_tokens, key_grad, other_key_grad, cos, sin, both
    )
    near = lax.all_to_all(partial.reshape(16, 256, kvw // 2), NEAR, 0, 0)
    near_sum = near_total(near.reshape(8, 2, 256, kvw // 2), blocks[3], blocks[7])
    far = lax.all_to_all(near_sum, FAR, 0, 0, tiled=True)
    summed = far.reshape(64, 4, kvw).astype(jnp.float32).sum(0)
    count = rows * math.prod(SIZES.values())
    weight_grad = (summed * (1.0 / math.sqrt(count))).astype(jnp.bfloat16)

    y = lax.axis_index(("yh", "yl"))
    p_own, p_other, t_own, t_other = forward(
        jnp.stack([core, y]),
        tokens,
        other_tokens,
        key_grad,
        other_key_grad,
        cos,
        sin,
        blocks,
        near_sum,
    )
    p_other = lax.ppermute(p_other, "c", SWAP)
    t_other = lax.ppermute(t_other, "c", SWAP)
    rotated, token_grad = finish(core.reshape(1), p_own, p_other, t_own, t_other, cos, sin)
    return (rotated, token_grad, weight_grad)


def solution(mesh):
    fine = Mesh(mesh.devices.reshape(tuple(SIZES.values())), tuple(SIZES))
    everywhere = P(REP + FSDP, None)
    return jax.shard_map(
        body,
        mesh=fine,
        in_specs=(everywhere, P(FSDP, None), P(FSDP), everywhere),
        out_specs=(everywhere, everywhere, everywhere),
        check_vma=False,
    )
```

time: 335 us -> 112 us (0.33)
  blocking collectives: 196 us -> 0 us
  waiting for transfers between devices: 84.8 us -> 12.8 us
  starting transfers between devices: 0.08 us -> 67.7 us
  between operations: 15.5 us -> 0.88 us
  matrix products: 13.7 us -> 0 us
  Pallas kernels: 0 us -> 11.2 us
  local copies, waits for them, and re-layouts: 24.1 us -> 16.6 us
    unnamed x2 -> x0, blocking collectives: 196 us -> none
    unnamed x3 -> x0, waiting for transfers between devices: 84.8 us -> none
    ppermute x0 -> x12, starting transfers between devices: none -> 34.8 us  [the longest x3 15.4 us: gather(): lefts.append(lax.ppermute(lefts[-1], axes, left))]
    all_to_all x0 -> x2, starting transfers between devices: none -> 32.9 us  [the longest x1 18.1 us: body(): near = lax.all_to_all(partial.reshape(16, 256, kvw // 2), NEAR, 0, 0)]
    dot_general x3 -> x0, matrix products: 13.7 us -> none  [the longest x1 5.47 us: body(): lax.dot_general(proj_grad, weight, (((1,), (1,)), ((), ())), preferred_el...]
    pallas_call x0 -> x6, Pallas kernels: none -> 11.2 us  [the longest x1 2.93 us: forward(): pl.pallas_call(forward_kernel, out_shape=[jax.ShapeDtypeStruct((rows, kvw...]
    ppermute x0 -> x12, waiting for transfers between devices: none -> 10.7 us  [the longest x4 7.83 us: gather(): rights.append(lax.ppermute(rights[-1], axes, right))]
    reshape x2 -> x0, local copies, waits for them, and re-layouts: 4.73 us -> none  [the longest x1 2.58 us: body(): reordered = tokens.reshape(row_count, rep_size, fsdp_size, share).transpo...]
  transfers between devices with their start and end apart: 2 -> 14, of which waited for: 1 -> 6; matrix products, arithmetic and copies ran while one was open for 2% -> 1% of each run, Pallas kernels for 0% -> 8%
where the time goes in v2:
time: 112 us; the launch traced here: 111 us
  starting transfers between devices  67.7 us (60%)
  local copies, waits for them, and re-layouts  16.6 us (15%)
  waiting for transfers between devices  12.8 us (11%)
  Pallas kernels  11.2 us (10%)
  other arithmetic  1.68 us (2%)
    all_to_all x1, starting transfers between devices, body(): near = lax.all_to_all(partial.reshape(16, 256, kvw // 2), NEAR, 0, 0)  18.1 us
    unnamed x38, local copies, waits for them, and re-layouts  15.8 us
    ppermute x3, starting transfers between devices, gather(): lefts.append(lax.ppermute(lefts[-1], axes, left))  15.4 us
    all_to_all x1, starting transfers between devices, body(): far = lax.all_to_all(near_sum, FAR, 0, 0, tiled=True)  14.8 us
    ppermute x4, waiting for transfers between devices, gather(): rights.append(lax.ppermute(rights[-1], axes, right))  7.83 us
    ppermute x4, starting transfers between devices, gather(): rights.append(lax.ppermute(rights[-1], axes, right))  7.65 us
    ppermute x1, starting transfers between devices, body(): across = lax.ppermute(shard, ('xl', 'xh'), [(i, 3 - i) for i in range(4)])  3.39 us
    pallas_call x1, Pallas kernels, forward(): pl.pallas_call(forward_kernel, out_shape=[jax.ShapeDtypeStruct((rows, kvw...  2.93 us
  transfers between devices with their start and end apart: 14, of which 6 were waited for; matrix products, arithmetic and copies ran while one was open for 1% of the time, Pallas kernels for 8%

profile of v2, /device:TPU:2, one launch (start us, length us, event | category | flops | bytes accessed | tf_op | source)
XLA Modules:
  0.0 110.8 jit_solution(4298585788411488705)
XLA Ops:
  0.6 1.9 %collective-permute-start = (bf16[192,4096]{1,0:T(8,128)(2,1)}, bf16[192,4096]{1,0:T(8,128)(2,1)S(1)}, u32[]{:S(2)}, u32[]{:S(2)}) collective-permute-start(bf16[192,4096]{1,0:T(8,128)(2,1)} %own.3), channel_id=1, source_target_pairs={{0,1},{1,0},{2,3},{3,2},{4,5},{5,4},{6,7},{7,6},{8,9},{9,8},{10,11... | collective-permute-start | bytes 4718600 | tf_op jit(solution)/shard_map/ppermute | solution.py:266
  2.6 1.7 %dequantize.1.own = bf16[128,512]{1,0:T(8,128)(2,1)} custom-call(bf16[1,32]{1,0:T(2,128)(2,1)} %bitcast.7, bf16[128,512]{1,0:T(8,128)(2,1)} %quant.1), custom_call_target="tpu_custom_call" | custom-call | tf_op jit(solution)/shard_map/dequantize/pallas_call | solution.py:35
  4.2 3.4 %collective-permute-start.2 = (bf16[128,512]{1,0:T(8,128)(2,1)}, bf16[128,512]{1,0:T(8,128)(2,1)S(1)}, u32[]{:S(2)}, u32[]{:S(2)}) collective-permute-start(bf16[128,512]{1,0:T(8,128)(2,1)} %dequantize.1.own), channel_id=1, source_target_pairs={{0,528},{16,512},{512,16},{528,0},{1,529},{17,513},{513,17},{529,1... | collective-permute-start | bytes 393224 | tf_op jit(solution)/shard_map/ppermute | solution.py:262
  7.6 2.1 %collective-permute-start.1 = (bf16[192,512]{1,0:T(8,128)(2,1)}, bf16[192,512]{1,0:T(8,128)(2,1)S(1)}, u32[]{:S(2)}, u32[]{:S(2)}) collective-permute-start(bf16[192,512]{1,0:T(8,128)(2,1)} %kg_own.3), channel_id=1, source_target_pairs={{0,1},{1,0},{2,3},{3,2},{4,5},{5,4},{6,7},{7,6},{8,9},{9,8},{10,11... | collective-permute-start | bytes 589832 | tf_op jit(solution)/shard_map/ppermute | solution.py:267
  10.7 1.6 %collective-permute-done.2.across = bf16[128,512]{1,0:T(8,128)(2,1)S(1)} collective-permute-done((bf16[128,512]{1,0:T(8,128)(2,1)}, bf16[128,512]{1,0:T(8,128)(2,1)S(1)}, u32[]{:S(2)}, u32[]{:S(2)}) %collective-permute-start.2) | collective-permute-done | bytes 131104 | tf_op jit(solution)/shard_map/ppermute | solution.py:262
  12.9 1.7 %pair.1.after.refs_0_ = bf16[2,128,512]{2,1,0:T(8,128)(2,1)} custom-call(s32[1]{0:T(128)} %bitcast.2.xh, bf16[128,512]{1,0:T(8,128)(2,1)} %dequantize.1.own, bf16[128,512]{1,0:T(8,128)(2,1)} %copy-done.18), custom_call_target="tpu_custom_call" | custom-call | tf_op jit(solution)/shard_map/pair/pallas_call | solution.py:49
  14.6 2.0 %copy-done = bf16[192,4096]{1,0:T(8,128)(2,1)S(1)} copy-done((bf16[192,4096]{1,0:T(8,128)(2,1)S(1)}, bf16[192,4096]{1,0:T(8,128)(2,1)}, u32[]{:S(2)}) %copy-start) | copy-done | bytes 1572888
  16.6 0.9 copy-done.4
  18.5 2.8 %weight_partial.1 = bf16[2,4,2,8,32,256]{5,4,3,2,1,0:T(8,128)(2,1)} custom-call(s32[1]{0:T(128)} %bitcast.core, bf16[192,4096]{1,0:T(8,128)(2,1)S(1)} %copy-done, bf16[192,4096]{1,0:T(8,128)(2,1)S(1)} %collective-permute-done.other, bf16[192,512]{1,0:T(8,128)(2,1)S(1)} %copy-done.6, bf16[192,512]{1,0:T(8,128)(2,1)S(1)} %collective-permute-done.1.kg_other, ...), custom_call_target="tpu_custom_call" | custom-call | tf_op jit(solution)/shard_map/weight_partial/pallas_call | solution.py:149
  21.3 18.1 %all-to-all-start = ((bf16[16,256,256]{2,1,0:T(8,128)(2,1)}), bf16[16,256,256]{2,1,0:T(8,128)(2,1)S(1)}, u32[]{:S(2)}, u32[]{:S(2)}) async-start(bf16[16,256,256]{2,1,0:T(8,128)(2,1)} %bitcast.4), calls=%async_computation | async-start | bytes 4194304 | tf_op jit(solution)/shard_map/all_to_all | solution.py:276
  39.4 1.9 %collective-permute-start.3 = (bf16[2,128,512]{2,1,0:T(8,128)(2,1)S(1)}, bf16[2,128,512]{2,1,0:T(8,128)(2,1)S(1)}, u32[]{:S(2)}, u32[]{:S(2)}) collective-permute-start(bf16[2,128,512]{2,1,0:T(8,128)(2,1)S(1)} %copy-done.5), channel_id=1, source_target_pairs={{0,2},{2,4},{4,6},{6,8},{8,10},{10,12},{12,14},{14,0},{1,3},{3,5},... | collective-permute-start | bytes 786440 | tf_op jit(solution)/shard_map/ppermute | solution.py:64
  41.3 5.1 %collective-permute-start.7 = (bf16[2,128,512]{2,1,0:T(8,128)(2,1)S(1)}, bf16[2,128,512]{2,1,0:T(8,128)(2,1)S(1)}, u32[]{:S(2)}, u32[]{:S(2)}) collective-permute-start(bf16[2,128,512]{2,1,0:T(8,128)(2,1)S(1)} %copy-done.5), channel_id=1, source_target_pairs={{0,14},{2,0},{4,2},{6,4},{8,6},{10,8},{12,10},{14,12},{1,15},{3,1}... | collective-permute-start | bytes 786440 | tf_op jit(solution)/shard_map/ppermute | solution.py:65
  46.5 4.4 %collective-permute-done.3.refs_1_ = bf16[2,128,512]{2,1,0:T(8,128)(2,1)S(1)} collective-permute-done((bf16[2,128,512]{2,1,0:T(8,128)(2,1)S(1)}, bf16[2,128,512]{2,1,0:T(8,128)(2,1)S(1)}, u32[]{:S(2)}, u32[]{:S(2)}) %collective-permute-start.3) | collective-permute-done | bytes 262176 | tf_op jit(solution)/shard_map/ppermute | solution.py:64
  50.9 1.9 %collective-permute-start.4 = (bf16[2,128,512]{2,1,0:T(8,128)(2,1)S(1)}, bf16[2,128,512]{2,1,0:T(8,128)(2,1)S(1)}, u32[]{:S(2)}, u32[]{:S(2)}) collective-permute-start(bf16[2,128,512]{2,1,0:T(8,128)(2,1)S(1)} %collective-permute-done.3.refs_1_), channel_id=1, source_target_pairs={{0,2},{2,4},{4,6},{6,8},{8,10},{10,12},{12,14},{14,0},{1,3},{3,5},... | collective-permute-start | bytes 786440 | tf_op jit(solution)/shard_map/ppermute | solution.py:64
  53.5 5.1 %collective-permute-start.8 = (bf16[2,128,512]{2,1,0:T(8,128)(2,1)S(1)}, bf16[2,128,512]{2,1,0:T(8,128)(2,1)S(1)}, u32[]{:S(2)}, u32[]{:S(2)}) collective-permute-start(bf16[2,128,512]{2,1,0:T(8,128)(2,1)S(1)} %collective-permute-done.7.refs_5_), channel_id=1, source_target_pairs={{0,14},{2,0},{4,2},{6,4},{8,6},{10,8},{12,10},{14,12},{1,15},{3,1}... | collective-permute-start | bytes 786440 | tf_op jit(solution)/shard_map/ppermute | solution.py:65
  59.3 2.2 %collective-permute-done.4.refs_2_ = bf16[2,128,512]{2,1,0:T(8,128)(2,1)S(1)} collective-permute-done((bf16[2,128,512]{2,1,0:T(8,128)(2,1)S(1)}, bf16[2,128,512]{2,1,0:T(8,128)(2,1)S(1)}, u32[]{:S(2)}, u32[]{:S(2)}) %collective-permute-start.4) | collective-permute-done | bytes 262176 | tf_op jit(solution)/shard_map/ppermute | solution.py:64
  61.5 1.9 %collective-permute-start.5 = (bf16[2,128,512]{2,1,0:T(8,128)(2,1)S(1)}, bf16[2,128,512]{2,1,0:T(8,128)(2,1)S(1)}, u32[]{:S(2)}, u32[]{:S(2)}) collective-permute-start(bf16[2,128,512]{2,1,0:T(8,128)(2,1)S(1)} %collective-permute-done.4.refs_2_), channel_id=1, source_target_pairs={{0,2},{2,4},{4,6},{6,8},{8,10},{10,12},{12,14},{14,0},{1,3},{3,5},... | collective-permute-start | bytes 786440 | tf_op jit(solution)/shard_map/ppermute | solution.py:64
  64.1 5.1 %collective-permute-start.9 = (bf16[2,128,512]{2,1,0:T(8,128)(2,1)S(1)}, bf16[2,128,512]{2,1,0:T(8,128)(2,1)S(1)}, u32[]{:S(2)}, u32[]{:S(2)}) collective-permute-start(bf16[2,128,512]{2,1,0:T(8,128)(2,1)S(1)} %collective-permute-done.8.refs_6_), channel_id=1, source_target_pairs={{0,14},{2,0},{4,2},{6,4},{8,6},{10,8},{12,10},{14,12},{1,15},{3,1}... | collective-permute-start | bytes 786440 | tf_op jit(solution)/shard_map/ppermute | solution.py:65
  70.0 1.3 %collective-permute-done.5.after_right.refs_3_ = bf16[2,128,512]{2,1,0:T(8,128)(2,1)S(1)} collective-permute-done((bf16[2,128,512]{2,1,0:T(8,128)(2,1)S(1)}, bf16[2,128,512]{2,1,0:T(8,128)(2,1)S(1)}, u32[]{:S(2)}, u32[]{:S(2)}) %collective-permute-start.5) | collective-permute-done | bytes 262176 | tf_op jit(solution)/shard_map/ppermute | solution.py:64
  71.2 1.9 %collective-permute-start.6 = (bf16[2,128,512]{2,1,0:T(8,128)(2,1)S(1)}, bf16[2,128,512]{2,1,0:T(8,128)(2,1)}, u32[]{:S(2)}, u32[]{:S(2)}) collective-permute-start(bf16[2,128,512]{2,1,0:T(8,128)(2,1)S(1)} %collective-permute-done.5.after_right.refs_3_), channel_id=1, source_target_pairs={{0,2},{2,4},{4,6},{6,8},{8,10},{10,12},{12,14},{14,0},{1,3},{3,5},... | collective-permute-start | bytes 786440 | tf_op jit(solution)/shard_map/ppermute | solution.py:66
  74.2 14.8 %all-to-all-start.1 = ((bf16[64,4,512]{2,1,0:T(4,128)(2,1)}), bf16[64,4,512]{2,1,0:T(4,128)(2,1)S(1)}, u32[]{:S(2)}, u32[]{:S(2)}) async-start(bf16[64,4,512]{2,1,0:T(4,128)(2,1)} %all_to_all.10), calls=%async_computation.1 | async-start | bytes 524288 | tf_op jit(solution)/shard_map/all_to_all | solution.py:278
  89.1 1.4 %copy-done.1 = bf16[192,4096]{1,0:T(8,128)(2,1)S(1)} copy-done((bf16[192,4096]{1,0:T(8,128)(2,1)S(1)}, bf16[192,4096]{1,0:T(8,128)(2,1)}, u32[]{:S(2)}) %copy-start.1) | copy-done | bytes 1572888
  90.5 1.4 %copy-done.3 = bf16[192,4096]{1,0:T(8,128)(2,1)S(1)} copy-done((bf16[192,4096]{1,0:T(8,128)(2,1)S(1)}, bf16[192,4096]{1,0:T(8,128)(2,1)}, u32[]{:S(2)}) %copy-start.3) | copy-done | bytes 1572888
  93.7 0.9 copy-done.11
  94.7 0.9 copy-done.13
  95.6 0.9 copy-done.15
  97.5 2.9 %forward.1 = (f32[192,512]{1,0:T(8,128)S(1)}, f32[192,512]{1,0:T(8,128)S(1)}, bf16[192,2048]{1,0:T(8,128)(2,1)S(1)}, bf16[192,2048]{1,0:T(8,128)(2,1)S(1)}) custom-call(s32[2]{0:T(128)S(1)} %pad_add_fusion.place, bf16[192,4096]{1,0:T(8,128)(2,1)S(1)} %copy-done.1, bf16[192,4096]{1,0:T(8,128)(2,1)S(1)} %copy-done.3, bf16[192,512]{1,0:T(8,128)(2,1)S(1)} %copy-done.7, ...), custom_call_target="tpu_custom_call" | custom-call | tf_op jit(solution)/shard_map/forward/pallas_call | solution.py:201
  100.5 1.9 %collective-permute-start.11 = (bf16[192,2048]{1,0:T(8,128)(2,1)S(1)}, bf16[192,2048]{1,0:T(8,128)(2,1)S(1)}, u32[]{:S(2)}, u32[]{:S(2)}) collective-permute-start(bf16[192,2048]{1,0:T(8,128)(2,1)S(1)} %get-tuple-element.12), channel_id=1, source_target_pairs={{0,1},{1,0},{2,3},{3,2},{4,5},{5,4},{6,7},{7,6},{8,9},{9,8},{10,11... | collective-permute-start | bytes 2359304 | tf_op jit(solution)/shard_map/ppermute | solution.py:296
  102.4 2.4 %collective-permute-start.10 = (f32[192,512]{1,0:T(8,128)S(1)}, f32[192,512]{1,0:T(8,128)S(1)}, u32[]{:S(2)}, u32[]{:S(2)}) collective-permute-start(f32[192,512]{1,0:T(8,128)S(1)} %get-tuple-element.10), channel_id=1, source_target_pairs={{0,1},{1,0},{2,3},{3,2},{4,5},{5,4},{6,7},{7,6},{8,9},{9,8},{10,11... | collective-permute-start | bytes 1179656 | tf_op jit(solution)/shard_map/ppermute | solution.py:295
  104.8 1.3 %collective-permute-done.10.p_other = f32[192,512]{1,0:T(8,128)S(1)} collective-permute-done((f32[192,512]{1,0:T(8,128)S(1)}, f32[192,512]{1,0:T(8,128)S(1)}, u32[]{:S(2)}, u32[]{:S(2)}) %collective-permute-start.10) | collective-permute-done | bytes 393248 | tf_op jit(solution)/shard_map/ppermute | solution.py:295
  106.1 1.9 %finish.1 = (bf16[192,512]{1,0:T(8,128)(2,1)}, bf16[192,4096]{1,0:T(8,128)(2,1)}) custom-call(s32[1]{0:T(128)} %bitcast.core, f32[192,512]{1,0:T(8,128)S(1)} %get-tuple-element.9.p_own, f32[192,512]{1,0:T(8,128)S(1)} %collective-permute-done.10.p_other, bf16[192,2048]{1,0:T(8,128)(2,1)S(1)} %get-tuple-element.11.t_own, ...), custom_call_target="tpu_custom_call" | custom-call | tf_op jit(solution)/shard_map/finish/pallas_call | solution.py:236
  108.0 2.1 %all-to-all-done.1 = bf16[64,4,512]{2,1,0:T(4,128)(2,1)S(1)} async-done(((bf16[64,4,512]{2,1,0:T(4,128)(2,1)}), bf16[64,4,512]{2,1,0:T(4,128)(2,1)S(1)}, u32[]{:S(2)}, u32[]{:S(2)}) %all-to-all-start.1) | async-done | bytes 262176 | tf_op jit(solution)/shard_map/all_to_all | solution.py:278
  (48 shorter events, 9.9 us)
Async XLA Ops:
  0.6 14.0 %collective-permute-start = (bf16[192,4096]{1,0:T(8,128)(2,1)}, bf16[192,4096]{1,0:T(8,128)(2,1)S(1)}, u32[]{:S(2)}, u32[]{:S(2)}) collective-permute-start(bf16[192,4096]{1,0:T(8,128)(2,1)} %own.3), channel_id=1, source_target_pairs={{0,1},{1,0},{2,3},{3,2},{4,5},{5,4},{6,7},{7,6},{8,9},{9,8},{10,11... | collective-permute-start | bytes 4718600 | tf_op jit(solution)/shard_map/ppermute | solution.py:266
  4.2 8.0 %collective-permute-start.2 = (bf16[128,512]{1,0:T(8,128)(2,1)}, bf16[128,512]{1,0:T(8,128)(2,1)S(1)}, u32[]{:S(2)}, u32[]{:S(2)}) collective-permute-start(bf16[128,512]{1,0:T(8,128)(2,1)} %dequantize.1.own), channel_id=1, source_target_pairs={{0,528},{16,512},{512,16},{528,0},{1,529},{17,513},{513,17},{529,1... | collective-permute-start | bytes 393224 | tf_op jit(solution)/shard_map/ppermute | solution.py:262
  7.6 6.9 %collective-permute-start.1 = (bf16[192,512]{1,0:T(8,128)(2,1)}, bf16[192,512]{1,0:T(8,128)(2,1)S(1)}, u32[]{:S(2)}, u32[]{:S(2)}) collective-permute-start(bf16[192,512]{1,0:T(8,128)(2,1)} %kg_own.3), channel_id=1, source_target_pairs={{0,1},{1,0},{2,3},{3,2},{4,5},{5,4},{6,7},{7,6},{8,9},{9,8},{10,11... | collective-permute-start | bytes 589832 | tf_op jit(solution)/shard_map/ppermute | solution.py:267
  14.6 6.8 %copy-start.8 = (bf16[192,512]{1,0:T(8,128)(2,1)}, bf16[192,512]{1,0:T(8,128)(2,1)S(1)}, u32[]{:S(2)}) copy-start(bf16[192,512]{1,0:T(8,128)(2,1)S(1)} %collective-permute-done.1.kg_other) | copy-start | bytes 589828
  14.6 6.8 %copy-start.2 = (bf16[192,4096]{1,0:T(8,128)(2,1)}, bf16[192,4096]{1,0:T(8,128)(2,1)S(1)}, u32[]{:S(2)}) copy-start(bf16[192,4096]{1,0:T(8,128)(2,1)S(1)} %collective-permute-done.other) | copy-start | bytes 4718596
  14.6 2.0 %copy-start = (bf16[192,4096]{1,0:T(8,128)(2,1)S(1)}, bf16[192,4096]{1,0:T(8,128)(2,1)}, u32[]{:S(2)}) copy-start(bf16[192,4096]{1,0:T(8,128)(2,1)} %own.3) | copy-start | bytes 4718596
  16.6 0.9 copy-start.4
  17.6 0.9 copy-start.6
  21.3 18.1 %copy-start.5 = (bf16[2,128,512]{2,1,0:T(8,128)(2,1)S(1)}, bf16[2,128,512]{2,1,0:T(8,128)(2,1)}, u32[]{:S(2)}) copy-start(bf16[2,128,512]{2,1,0:T(8,128)(2,1)} %pair.1.after.refs_0_) | copy-start | bytes 786436
  21.3 51.8 %all-to-all-start = ((bf16[16,256,256]{2,1,0:T(8,128)(2,1)}), bf16[16,256,256]{2,1,0:T(8,128)(2,1)S(1)}, u32[]{:S(2)}, u32[]{:S(2)}) async-start(bf16[16,256,256]{2,1,0:T(8,128)(2,1)} %bitcast.4), calls=%async_computation | async-start | bytes 4194304 | tf_op jit(solution)/shard_map/all_to_all | solution.py:276
  39.4 11.5 %collective-permute-start.3 = (bf16[2,128,512]{2,1,0:T(8,128)(2,1)S(1)}, bf16[2,128,512]{2,1,0:T(8,128)(2,1)S(1)}, u32[]{:S(2)}, u32[]{:S(2)}) collective-permute-start(bf16[2,128,512]{2,1,0:T(8,128)(2,1)S(1)} %copy-done.5), channel_id=1, source_target_pairs={{0,2},{2,4},{4,6},{6,8},{8,10},{10,12},{12,14},{14,0},{1,3},{3,5},... | collective-permute-start | bytes 786440 | tf_op jit(solution)/shard_map/ppermute | solution.py:64
  41.3 12.2 %collective-permute-start.7 = (bf16[2,128,512]{2,1,0:T(8,128)(2,1)S(1)}, bf16[2,128,512]{2,1,0:T(8,128)(2,1)S(1)}, u32[]{:S(2)}, u32[]{:S(2)}) collective-permute-start(bf16[2,128,512]{2,1,0:T(8,128)(2,1)S(1)} %copy-done.5), channel_id=1, source_target_pairs={{0,14},{2,0},{4,2},{6,4},{8,6},{10,8},{12,10},{14,12},{1,15},{3,1}... | collective-permute-start | bytes 786440 | tf_op jit(solution)/shard_map/ppermute | solution.py:65
  50.9 10.6 %collective-permute-start.4 = (bf16[2,128,512]{2,1,0:T(8,128)(2,1)S(1)}, bf16[2,128,512]{2,1,0:T(8,128)(2,1)S(1)}, u32[]{:S(2)}, u32[]{:S(2)}) collective-permute-start(bf16[2,128,512]{2,1,0:T(8,128)(2,1)S(1)} %collective-permute-done.3.refs_1_), channel_id=1, source_target_pairs={{0,2},{2,4},{4,6},{6,8},{8,10},{10,12},{12,14},{14,0},{1,3},{3,5},... | collective-permute-start | bytes 786440 | tf_op jit(solution)/shard_map/ppermute | solution.py:64
  52.8 0.7 copy-start.10
  53.5 10.6 %collective-permute-start.8 = (bf16[2,128,512]{2,1,0:T(8,128)(2,1)S(1)}, bf16[2,128,512]{2,1,0:T(8,128)(2,1)S(1)}, u32[]{:S(2)}, u32[]{:S(2)}) collective-permute-start(bf16[2,128,512]{2,1,0:T(8,128)(2,1)S(1)} %collective-permute-done.7.refs_5_), channel_id=1, source_target_pairs={{0,14},{2,0},{4,2},{6,4},{8,6},{10,8},{12,10},{14,12},{1,15},{3,1}... | collective-permute-start | bytes 786440 | tf_op jit(solution)/shard_map/ppermute | solution.py:65
  58.6 0.7 copy-start.12
  61.5 9.7 %collective-permute-start.5 = (bf16[2,128,512]{2,1,0:T(8,128)(2,1)S(1)}, bf16[2,128,512]{2,1,0:T(8,128)(2,1)S(1)}, u32[]{:S(2)}, u32[]{:S(2)}) collective-permute-start(bf16[2,128,512]{2,1,0:T(8,128)(2,1)S(1)} %collective-permute-done.4.refs_2_), channel_id=1, source_target_pairs={{0,2},{2,4},{4,6},{6,8},{8,10},{10,12},{12,14},{14,0},{1,3},{3,5},... | collective-permute-start | bytes 786440 | tf_op jit(solution)/shard_map/ppermute | solution.py:64
  63.4 0.7 copy-start.14
  64.1 9.0 %collective-permute-start.9 = (bf16[2,128,512]{2,1,0:T(8,128)(2,1)S(1)}, bf16[2,128,512]{2,1,0:T(8,128)(2,1)S(1)}, u32[]{:S(2)}, u32[]{:S(2)}) collective-permute-start(bf16[2,128,512]{2,1,0:T(8,128)(2,1)S(1)} %collective-permute-done.8.refs_6_), channel_id=1, source_target_pairs={{0,14},{2,0},{4,2},{6,4},{8,6},{10,8},{12,10},{14,12},{1,15},{3,1}... | collective-permute-start | bytes 786440 | tf_op jit(solution)/shard_map/ppermute | solution.py:65
  69.3 0.7 copy-start.16
  71.2 17.8 %collective-permute-start.6 = (bf16[2,128,512]{2,1,0:T(8,128)(2,1)S(1)}, bf16[2,128,512]{2,1,0:T(8,128)(2,1)}, u32[]{:S(2)}, u32[]{:S(2)}) collective-permute-start(bf16[2,128,512]{2,1,0:T(8,128)(2,1)S(1)} %collective-permute-done.5.after_right.refs_3_), channel_id=1, source_target_pairs={{0,2},{2,4},{4,6},{6,8},{8,10},{10,12},{12,14},{14,0},{1,3},{3,5},... | collective-permute-start | bytes 786440 | tf_op jit(solution)/shard_map/ppermute | solution.py:66
  74.2 35.9 %all-to-all-start.1 = ((bf16[64,4,512]{2,1,0:T(4,128)(2,1)}), bf16[64,4,512]{2,1,0:T(4,128)(2,1)S(1)}, u32[]{:S(2)}, u32[]{:S(2)}) async-start(bf16[64,4,512]{2,1,0:T(4,128)(2,1)} %all_to_all.10), calls=%async_computation.1 | async-start | bytes 524288 | tf_op jit(solution)/shard_map/all_to_all | solution.py:278
  89.1 1.4 %copy-start.1 = (bf16[192,4096]{1,0:T(8,128)(2,1)S(1)}, bf16[192,4096]{1,0:T(8,128)(2,1)}, u32[]{:S(2)}) copy-start(bf16[192,4096]{1,0:T(8,128)(2,1)} %own.3) | copy-start | bytes 4718596
  90.5 1.4 %copy-start.3 = (bf16[192,4096]{1,0:T(8,128)(2,1)S(1)}, bf16[192,4096]{1,0:T(8,128)(2,1)}, u32[]{:S(2)}) copy-start(bf16[192,4096]{1,0:T(8,128)(2,1)} %copy-done.2) | copy-start | bytes 4718596
  91.9 0.9 copy-start.7
  92.8 0.9 copy-start.9
  93.7 0.9 copy-start.11
  94.7 0.9 copy-start.13
  95.6 0.9 copy-start.15
  96.6 0.9 copy-start.17
  100.5 5.7 %collective-permute-start.11 = (bf16[192,2048]{1,0:T(8,128)(2,1)S(1)}, bf16[192,2048]{1,0:T(8,128)(2,1)S(1)}, u32[]{:S(2)}, u32[]{:S(2)}) collective-permute-start(bf16[192,2048]{1,0:T(8,128)(2,1)S(1)} %get-tuple-element.12), channel_id=1, source_target_pairs={{0,1},{1,0},{2,3},{3,2},{4,5},{5,4},{6,7},{7,6},{8,9},{9,8},{10,11... | collective-permute-start | bytes 2359304 | tf_op jit(solution)/shard_map/ppermute | solution.py:296
  102.4 3.7 %collective-permute-start.10 = (f32[192,512]{1,0:T(8,128)S(1)}, f32[192,512]{1,0:T(8,128)S(1)}, u32[]{:S(2)}, u32[]{:S(2)}) collective-permute-start(f32[192,512]{1,0:T(8,128)S(1)} %get-tuple-element.10), channel_id=1, source_target_pairs={{0,1},{1,0},{2,3},{3,2},{4,5},{5,4},{6,7},{7,6},{8,9},{9,8},{10,11... | collective-permute-start | bytes 1179656 | tf_op jit(solution)/shard_map/ppermute | solution.py:295
  (1 other events, 0.7 us)

commit v3 on v2

--- a/solution.py
+++ b/solution.py
@@ -18,7 +18,8 @@
 NEAR = ("xl", "zl", "xh", "c")
 FAR = ("zh", "yh", "yl")
 SWAP = [(0, 1), (1, 0)]
-GRANT = 32 * 2**20
+GRANT = 8 * 2**20
+WIDE = 56 * 2**20
 QUICK = pl.CostEstimate(flops=0, bytes_accessed=0, transcendentals=0)
 
 
@@ -35,24 +36,33 @@
     return pl.pallas_call(
         dequantize_kernel,
         out_shape=jax.ShapeDtypeStruct(quant_weight.shape, jnp.bfloat16),
+        compiler_params=pltpu.CompilerParams(vmem_limit_bytes=GRANT),
+        cost_estimate=QUICK,
         name="dequantize",
     )(block_scales.reshape(1, -1), quant_weight)
 
 
-def pair_kernel(xh, own, across, out):
-    out[xh[0]] = own[...]
-    out[1 - xh[0]] = across[...]
-
-
-def pair(xh, own, across):
+def pair_kernel(here, own, across, passed, out, passed_on):
+    out[here[0]] = own[...]
+    out[1 - here[0]] = across[...]
+
+
+def pair(here, own, across, passed):
     vmem = pl.BlockSpec(memory_space=pltpu.VMEM)
+    anywhere = pl.BlockSpec(memory_space=pl.ANY)
     return pl.pallas_call(
         pair_kernel,
-        out_shape=jax.ShapeDtypeStruct((2,) + own.shape, own.dtype),
-        in_specs=[pl.BlockSpec(memory_space=pltpu.SMEM), vmem, vmem],
-        out_specs=vmem,
+        out_shape=(
+            jax.ShapeDtypeStruct((2,) + own.shape, own.dtype),
+            jax.ShapeDtypeStruct(passed.shape, passed.dtype),
+        ),
+        in_specs=[pl.BlockSpec(memory_space=pltpu.SMEM), vmem, vmem, anywhere],
+        out_specs=(vmem, anywhere),
+        input_output_aliases={3: 1},
+        compiler_params=pltpu.CompilerParams(vmem_limit_bytes=GRANT),
+        cost_estimate=QUICK,
         name="pair",
-    )(xh.reshape(1), own, across)
+    )(here, own, across, passed)
 
 
 def gather(across_xh):
@@ -110,7 +120,7 @@
     return parts
 
 
-def grad_kernel(core, own, other, kg_own, kg_other, cos, sin, after, out, proj_grad):
+def grad_kernel(core, own, other, kg_own, kg_other, cos, sin, out, proj_grad):
     rows, features = own.shape
     width = proj_grad.shape[1]
     mine = pl.multiple_of(core[0] * width, width)
@@ -142,81 +152,125 @@
             out[xl, k, 1, zh] = jnp.concatenate(second, 0).astype(jnp.bfloat16)
 
 
-def weight_partial(core, own, other, kg_own, kg_other, cos, sin, after):
+def weight_partial(core, own, other, kg_own, kg_other, cos, sin):
     rows, features = own.shape
     kvw = kg_own.shape[1]
     vmem = pl.BlockSpec(memory_space=pltpu.VMEM)
     return pl.pallas_call(
         grad_kernel,
         out_shape=jax.ShapeDtypeStruct((2, 4, 2, 8, 32, kvw // 2), jnp.bfloat16),
-        in_specs=[pl.BlockSpec(memory_space=pltpu.SMEM)]
-        + [vmem] * 6
-        + [pl.BlockSpec(memory_space=pl.ANY)],
+        in_specs=[pl.BlockSpec(memory_space=pltpu.SMEM)] + [vmem] * 6,
         out_specs=vmem,
         scratch_shapes=[pltpu.VMEM((2 * rows, kvw // 2), jnp.bfloat16)],
         compiler_params=pltpu.CompilerParams(vmem_limit_bytes=GRANT),
-        cost_estimate=QUICK,
+        cost_estimate=pl.CostEstimate(
+            flops=2 * rows * features * kvw, bytes_accessed=8 * 2**20, transcendentals=0
+        ),
         name="weight_partial",
-    )(core, own, other, kg_own, kg_other, cos, sin, after)
-
-
-def forward_kernel(
-    place, own, other, kg_own, kg_other, cos, sin, *refs
-):
-    blocks, (after, p_own, p_other, t_own, t_other, proj_grad, total) = refs[:8], refs[8:]
+    )(core, own, other, kg_own, kg_other, cos, sin)
+
+
+def forward_kernel(place, own, other, kg_own, kg_other, cos, sin, *refs):
+    blocks, (after, p_out, t_out, p_sent, t_sent) = refs[:8], refs[8:13]
+    t_own, t_other, held, kg, weights, proj_grad, total, sems = refs[13:]
     rows, kvw = kg_own.shape
     core, y = place[0], place[1]
-    for k, source in enumerate((kg_own, kg_other)):
+    part = rows // 4
+    pairs = [(kg_own, kg.at[pl.ds(0, rows)]), (kg_other, kg.at[pl.ds(rows, rows)])]
+    pairs += [(block, weights.at[k]) for k, block in enumerate(blocks)]
+    pairs += [
+        (source.at[pl.ds(q * part, part)], held.at[pl.ds(k * rows + q * part, part)])
+        for k, source in enumerate((own, other))
+        for q in range(4)
+    ]
+    loads = [pltpu.make_async_copy(a, b, sems.at[i]) for i, (a, b) in enumerate(pairs)]
+    for copy in loads:
+        copy.start()
+    for k in range(2):
         at = pl.ds(k * rows, rows)
-        parts = turn(source[...].astype(jnp.float32), cos[at, :], -sin[at, :], kvw // HEAD_DIM)
-        for h, part in enumerate(parts):
-            proj_grad[at, h * HEAD_DIM : (h + 1) * HEAD_DIM] = part.astype(jnp.bfloat16)
-    for k, block in enumerate(blocks):
-        there = lax.rem(y + (8 - k if k <= 4 else k - 4), 8)
-        weight = block[...].reshape(256, kvw)
-        taken = []
-        for source in (own, other):
-            halves = [
-                source[:, pl.ds(pl.multiple_of((xh * 8 + there) * 256 + core * 128, 128), 128)]
-                for xh in range(2)
-            ]
-            taken.append(jnp.concatenate(halves, 1))
-        share = jnp.dot(jnp.concatenate(taken, 0), weight, preferred_element_type=jnp.float32)
-        total[...] = share if k == 0 else total[...] + share
+        loads[k].wait()
+        parts = turn(kg[at, :].astype(jnp.float32), cos[at, :], -sin[at, :], kvw // HEAD_DIM)
+        for h, p in enumerate(parts):
+            proj_grad[at, h * HEAD_DIM : (h + 1) * HEAD_DIM] = p.astype(jnp.bfloat16)
+
+    def column(k, xh):
+        return xh * 8 + lax.rem(y + (8 - k if k <= 4 else k - 4), 8)
+
+    for k in range(8):
+        loads[2 + k].wait()
         back = lax.dot_general(
-            proj_grad[...], weight, (((1,), (1,)), ((), ())), preferred_element_type=jnp.float32
+            proj_grad[...],
+            weights[k].reshape(256, kvw),
+            (((1,), (1,)), ((), ())),
+            preferred_element_type=jnp.float32,
         ).astype(jnp.bfloat16)
         for xh in range(2):
-            at = pl.ds(pl.multiple_of((xh * 8 + there) * 128, 128), 128)
-            t_own[:, at] = back[:rows, xh * 128 : (xh + 1) * 128]
-            t_other[:, at] = back[rows:, xh * 128 : (xh + 1) * 128]
-    p_own[...] = total[:rows]
-    p_other[...] = total[rows:]
+            at = pl.ds(pl.multiple_of(column(k, xh) * 128, 128), 128)
+            half = slice(xh * 128, (xh + 1) * 128)
+            t_own[:, at] = back[:rows, half]
+            t_other[:, at] = back[rows:, half]
+    stores = [
+        pltpu.make_async_copy(t_other, t_sent, sems.at[0]),
+        pltpu.make_async_copy(t_own, t_out, sems.at[1]),
+        pltpu.make_async_copy(total.at[pl.ds(rows, rows)], p_sent, sems.at[2]),
+        pltpu.make_async_copy(total.at[pl.ds(0, rows)], p_out, sems.at[3]),
+    ]
+    for store in stores[:2]:
+        store.start()
+    for copy in loads[10:]:
+        copy.wait()
+    for k in range(8):
+        taken = [
+            held[:, pl.ds(pl.multiple_of(column(k, xh) * 256 + core * 128, 128), 128)]
+            for xh in range(2)
+        ]
+        share = jnp.dot(
+            jnp.concatenate(taken, 1),
+            weights[k].reshape(256, kvw),
+            preferred_element_type=jnp.float32,
+        )
+        total[...] = share if k == 0 else total[...] + share
+    for store in stores[2:]:
+        store.start()
+    for copy in stores:
+        copy.wait()
 
 
 def forward(place, own, other, kg_own, kg_other, cos, sin, blocks, after):
     rows, features = own.shape
     kvw = kg_own.shape[1]
     vmem = pl.BlockSpec(memory_space=pltpu.VMEM)
+    anywhere = pl.BlockSpec(memory_space=pl.ANY)
     return pl.pallas_call(
         forward_kernel,
-        out_shape=[jax.ShapeDtypeStruct((rows, kvw), jnp.float32)] * 2
-        + [jax.ShapeDtypeStruct((rows, features // 2), jnp.bfloat16)] * 2,
+        out_shape=(
+            jax.ShapeDtypeStruct((rows, kvw), jnp.float32),
+            jax.ShapeDtypeStruct((rows, features // 2), jnp.bfloat16),
+            jax.ShapeDtypeStruct((rows, kvw), jnp.float32),
+            jax.ShapeDtypeStruct((rows, features // 2), jnp.bfloat16),
+        ),
         in_specs=[pl.BlockSpec(memory_space=pltpu.SMEM)]
-        + [vmem] * 14
-        + [pl.BlockSpec(memory_space=pl.ANY)],
-        out_specs=[vmem] * 4,
+        + [anywhere] * 4
+        + [vmem] * 2
+        + [anywhere] * 9,
+        out_specs=[anywhere] * 4,
         scratch_shapes=[
+            pltpu.VMEM((rows, features // 2), jnp.bfloat16),
+            pltpu.VMEM((rows, features // 2), jnp.bfloat16),
+            pltpu.VMEM((2 * rows, features), jnp.bfloat16),
+            pltpu.VMEM((2 * rows, kvw), jnp.bfloat16),
+            pltpu.VMEM((8,) + blocks[0].shape, jnp.bfloat16),
             pltpu.VMEM((2 * rows, kvw), jnp.bfloat16),
             pltpu.VMEM((2 * rows, kvw), jnp.float32),
+            pltpu.SemaphoreType.DMA((18,)),
         ],
-        compiler_params=pltpu.CompilerParams(vmem_limit_bytes=GRANT),
+        compiler_params=pltpu.CompilerParams(vmem_limit_bytes=WIDE),
         cost_estimate=QUICK,
         name="forward",
     )(place, own, other, kg_own, kg_other, cos, sin, *blocks, after)
 
 
-def finish_kernel(core, p_own, p_other, t_own, t_other, cos, sin, rotated, token_grad):
+def finish_kernel(core, p_own, t_own, p_other, t_other, cos, sin, rotated, token_grad):
     kvw = p_own.shape[1]
     total = p_own[...] + p_other[...]
     for h, part in enumerate(turn(total, cos[...], sin[...], kvw // HEAD_DIM)):
@@ -228,7 +282,7 @@
             token_grad[:, pl.ds(column, 128)] = source[:, at]
 
 
-def finish(core, p_own, p_other, t_own, t_other, cos, sin):
+def finish(core, p_own, t_own, p_other, t_other, cos, sin):
     rows, kvw = p_own.shape
     features = 2 * t_own.shape[1]
     steps = 3
@@ -241,14 +295,13 @@
             jax.ShapeDtypeStruct((rows, features), jnp.bfloat16),
         ),
         in_specs=[pl.BlockSpec(memory_space=pltpu.SMEM)]
-        + [block(kvw)] * 2
-        + [block(features // 2)] * 2
+        + [block(kvw), block(features // 2)] * 2
         + [block(HEAD_DIM)] * 2,
         out_specs=(block(kvw), block(features)),
-        compiler_params=pltpu.CompilerParams(vmem_limit_bytes=GRANT),
+        compiler_params=pltpu.CompilerParams(vmem_limit_bytes=WIDE),
         cost_estimate=QUICK,
         name="finish",
-    )(core, p_own, p_other, t_own, t_other, cos, sin)
+    )(core, p_own, t_own, p_other, t_other, cos, sin)
 
 
 def body(tokens, quant_weight, block_scales, key_grad):
@@ -260,9 +313,6 @@
 
     shard = dequantize(quant_weight, block_scales)
     across = lax.ppermute(shard, ("xl", "xh"), [(i, 3 - i) for i in range(4)])
-    both = pair(xh, shard, across)
-    blocks = gather(both)
-
     other_tokens = lax.ppermute(tokens, "c", SWAP)
     other_key_grad = lax.ppermute(key_grad, "c", SWAP)
 
@@ -271,30 +321,24 @@
     cos, sin = tables(positions)
 
     partial = weight_partial(
-        core.reshape(1), tokens, other_tokens, key_grad, other_key_grad, cos, sin, both
+        core.reshape(1), tokens, other_tokens, key_grad, other_key_grad, cos, sin
     )
+    both, partial = pair(xh.reshape(1), shard, across, partial)
+    blocks = gather(both)
     near = lax.all_to_all(partial.reshape(16, 256, kvw // 2), NEAR, 0, 0)
     near_sum = near_total(near.reshape(8, 2, 256, kvw // 2), blocks[3], blocks[7])
     far = lax.all_to_all(near_sum, FAR, 0, 0, tiled=True)
     summed = far.reshape(64, 4, kvw).astype(jnp.float32).sum(0)
     count = rows * math.prod(SIZES.values())
+
+    where = jnp.stack([core, lax.axis_index(("yh", "yl"))])
+    p_own, t_own, p_sent, t_sent = forward(
+        where, tokens, other_tokens, key_grad, other_key_grad, cos, sin, blocks, near_sum
+    )
+    p_other = lax.ppermute(p_sent, "c", SWAP)
+    t_other = lax.ppermute(t_sent, "c", SWAP)
+    rotated, token_grad = finish(core.reshape(1), p_own, t_own, p_other, t_other, cos, sin)
     weight_grad = (summed * (1.0 / math.sqrt(count))).astype(jnp.bfloat16)
-
-    y = lax.axis_index(("yh", "yl"))
-    p_own, p_other, t_own, t_other = forward(
-        jnp.stack([core, y]),
-        tokens,
-        other_tokens,
-        key_grad,
-        other_key_grad,
-        cos,
-        sin,
-        blocks,
-        near_sum,
-    )
-    p_other = lax.ppermute(p_other, "c", SWAP)
-    t_other = lax.ppermute(t_other, "c", SWAP)
-    rotated, token_grad = finish(core.reshape(1), p_own, p_other, t_own, t_other, cos, sin)
     return (rotated, token_grad, weight_grad)
 
 

time: 112 us -> 106 us (0.946)
  local copies, waits for them, and re-layouts: 16.6 us -> 6.41 us
  Pallas kernels: 11.2 us -> 14.4 us
  waiting for transfers between devices: 12.8 us -> 15.3 us
  starting transfers between devices: 67.7 us -> 65.7 us
    unnamed x38 -> x36, local copies, waits for them, and re-layouts: 15.8 us -> 5.62 us
    pallas_call x2, Pallas kernels: 4.61 us -> 7.46 us  [the longest x1 7.44 us: forward(): pl.pallas_call(forward_kernel, out_shape=(jax.ShapeDtypeStruct((rows, kvw...]
    ppermute x4, waiting for transfers between devices: 7.83 us -> 10.6 us  [gather(): rights.append(lax.ppermute(rights[-1], axes, right))]
    pallas_call x1, Pallas kernels: 1.85 us -> 3.72 us  [finish(): pl.pallas_call(finish_kernel, grid=(steps,), out_shape=(jax.ShapeDtypeStr...]
    all_to_all x1, starting transfers between devices: 18.1 us -> 16.2 us  [body(): near = lax.all_to_all(partial.reshape(16, 256, kvw // 2), NEAR, 0, 0)]
    pallas_call x1, Pallas kernels: 1.68 us -> 0.1 us  [dequantize(): pl.pallas_call(dequantize_kernel, out_shape=jax.ShapeDtypeStruct(quant_we...]
    ppermute x1, waiting for transfers between devices: 1.57 us -> 0.01 us  [body(): across = lax.ppermute(shard, ('xl', 'xh'), [(i, 3 - i) for i in range(4)])]
  transfers between devices with their start and end apart: 14 -> 14, of which waited for: 6 -> 6; matrix products, arithmetic and copies ran while one was open for 1% -> 1% of each run, Pallas kernels for 8% -> 14%
where the time goes in v3:
time: 106 us; the launch traced here: 105 us
  starting transfers between devices  65.7 us (62%)
  waiting for transfers between devices  15.3 us (14%)
  Pallas kernels  14.4 us (14%)
  local copies, waits for them, and re-layouts  6.41 us (6%)
  other arithmetic  2.2 us (2%)
    all_to_all x1, starting transfers between devices, body(): near = lax.all_to_all(partial.reshape(16, 256, kvw // 2), NEAR, 0, 0)  16.2 us
    ppermute x3, starting transfers between devices, gather(): lefts.append(lax.ppermute(lefts[-1], axes, left))  15.4 us
    all_to_all x1, starting transfers between devices, body(): far = lax.all_to_all(near_sum, FAR, 0, 0, tiled=True)  14.7 us
    ppermute x4, waiting for transfers between devices, gather(): rights.append(lax.ppermute(rights[-1], axes, right))  10.6 us
    ppermute x4, starting transfers between devices, gather(): rights.append(lax.ppermute(rights[-1], axes, right))  7.64 us
    pallas_call x1, Pallas kernels, forward(): pl.pallas_call(forward_kernel, out_shape=(jax.ShapeDtypeStruct((rows, kvw...  7.44 us
    unnamed x36, local copies, waits for them, and re-layouts  5.62 us
    pallas_call x1, Pallas kernels, finish(): pl.pallas_call(finish_kernel, grid=(steps,), out_shape=(jax.ShapeDtypeStr...  3.72 us
  transfers between devices with their start and end apart: 14, of which 6 were waited for; matrix products, arithmetic and copies ran while one was open for 1% of the time, Pallas kernels for 14%

profile of v3, /device:TPU:2, one launch (start us, length us, event | category | flops | bytes accessed | tf_op | source)
XLA Modules:
  0.0 105.0 jit_solution(5493560513425465002)
XLA Ops:
  0.6 1.9 %collective-permute-start = (bf16[192,4096]{1,0:T(8,128)(2,1)}, bf16[192,4096]{1,0:T(8,128)(2,1)S(1)}, u32[]{:S(2)}, u32[]{:S(2)}) collective-permute-start(bf16[192,4096]{1,0:T(8,128)(2,1)} %own.3), channel_id=1, source_target_pairs={{0,1},{1,0},{2,3},{3,2},{4,5},{5,4},{6,7},{7,6},{8,9},{9,8},{10,11... | collective-permute-start | bytes 4718600 | tf_op jit(solution)/shard_map/ppermute | solution.py:316
  2.6 0.9 copy-done.10
  3.5 0.7 copy-done.11
  4.2 3.4 %collective-permute-start.2 = (bf16[128,512]{1,0:T(8,128)(2,1)S(1)}, bf16[128,512]{1,0:T(8,128)(2,1)S(1)}, u32[]{:S(2)}, u32[]{:S(2)}) collective-permute-start(bf16[128,512]{1,0:T(8,128)(2,1)S(1)} %dequantize.1.own), channel_id=1, source_target_pairs={{0,528},{16,512},{512,16},{528,0},{1,529},{17,513},{513,17},{529,1... | collective-permute-start | bytes 393224 | tf_op jit(solution)/shard_map/ppermute | solution.py:315
  7.6 2.1 %collective-permute-start.1 = (bf16[192,512]{1,0:T(8,128)(2,1)}, bf16[192,512]{1,0:T(8,128)(2,1)S(1)}, u32[]{:S(2)}, u32[]{:S(2)}) collective-permute-start(bf16[192,512]{1,0:T(8,128)(2,1)} %kg_own.3), channel_id=1, source_target_pairs={{0,1},{1,0},{2,3},{3,2},{4,5},{5,4},{6,7},{7,6},{8,9},{9,8},{10,11... | collective-permute-start | bytes 589832 | tf_op jit(solution)/shard_map/ppermute | solution.py:317
  9.9 0.8 fusion
  10.7 0.5 collective-permute-done.1.kg_other
  11.2 2.0 %copy-done = bf16[192,4096]{1,0:T(8,128)(2,1)S(1)} copy-done((bf16[192,4096]{1,0:T(8,128)(2,1)S(1)}, bf16[192,4096]{1,0:T(8,128)(2,1)}, u32[]{:S(2)}) %copy-start) | copy-done | bytes 1572888
  13.2 0.9 copy-done.7
  14.2 2.8 %weight_partial.1.passed = bf16[2,4,2,8,32,256]{5,4,3,2,1,0:T(8,128)(2,1)} custom-call(s32[1]{0:T(128)} %bitcast.core, bf16[192,4096]{1,0:T(8,128)(2,1)S(1)} %copy-done, bf16[192,4096]{1,0:T(8,128)(2,1)S(1)} %collective-permute-done.other, bf16[192,512]{1,0:T(8,128)(2,1)S(1)} %copy-done.7, bf16[192,512]{1,0:T(8,128)(2,1)S(1)} %collective-permute-done.1.kg_other, ...), custom_call_target="tpu_custom_call" | custom-call | flops 805306368 | bytes 8388608 | tf_op jit(solution)/shard_map/weight_partial/pallas_call | solution.py:159
  17.0 16.2 %all-to-all-start = ((bf16[16,256,256]{2,1,0:T(8,128)(2,1)}), bf16[16,256,256]{2,1,0:T(8,128)(2,1)S(1)}, u32[]{:S(2)}, u32[]{:S(2)}) async-start(bf16[16,256,256]{2,1,0:T(8,128)(2,1)} %bitcast.4), calls=%async_computation | async-start | bytes 4194304 | tf_op jit(solution)/shard_map/all_to_all | solution.py:328
  33.3 1.9 %collective-permute-start.3 = (bf16[2,128,512]{2,1,0:T(8,128)(2,1)S(1)}, bf16[2,128,512]{2,1,0:T(8,128)(2,1)S(1)}, u32[]{:S(2)}, u32[]{:S(2)}) collective-permute-start(bf16[2,128,512]{2,1,0:T(8,128)(2,1)S(1)} %get-tuple-element.11.refs_0_), channel_id=1, source_target_pairs={{0,2},{2,4},{4,6},{6,8},{8,10},{10,12},{12,14},{14,0},{1,3},{3,5},... | collective-permute-start | bytes 786440 | tf_op jit(solution)/shard_map/ppermute | solution.py:74
  35.2 5.1 %collective-permute-start.7 = (bf16[2,128,512]{2,1,0:T(8,128)(2,1)S(1)}, bf16[2,128,512]{2,1,0:T(8,128)(2,1)S(1)}, u32[]{:S(2)}, u32[]{:S(2)}) collective-permute-start(bf16[2,128,512]{2,1,0:T(8,128)(2,1)S(1)} %get-tuple-element.11.refs_0_), channel_id=1, source_target_pairs={{0,14},{2,0},{4,2},{6,4},{8,6},{10,8},{12,10},{14,12},{1,15},{3,1}... | collective-permute-start | bytes 786440 | tf_op jit(solution)/shard_map/ppermute | solution.py:75
  40.3 4.4 %collective-permute-done.3.refs_1_ = bf16[2,128,512]{2,1,0:T(8,128)(2,1)S(1)} collective-permute-done((bf16[2,128,512]{2,1,0:T(8,128)(2,1)S(1)}, bf16[2,128,512]{2,1,0:T(8,128)(2,1)S(1)}, u32[]{:S(2)}, u32[]{:S(2)}) %collective-permute-start.3) | collective-permute-done | bytes 262176 | tf_op jit(solution)/shard_map/ppermute | solution.py:74
  44.7 1.9 %collective-permute-start.4 = (bf16[2,128,512]{2,1,0:T(8,128)(2,1)S(1)}, bf16[2,128,512]{2,1,0:T(8,128)(2,1)S(1)}, u32[]{:S(2)}, u32[]{:S(2)}) collective-permute-start(bf16[2,128,512]{2,1,0:T(8,128)(2,1)S(1)} %collective-permute-done.3.refs_1_), channel_id=1, source_target_pairs={{0,2},{2,4},{4,6},{6,8},{8,10},{10,12},{12,14},{14,0},{1,3},{3,5},... | collective-permute-start | bytes 786440 | tf_op jit(solution)/shard_map/ppermute | solution.py:74
  46.7 5.1 %collective-permute-start.8 = (bf16[2,128,512]{2,1,0:T(8,128)(2,1)S(1)}, bf16[2,128,512]{2,1,0:T(8,128)(2,1)S(1)}, u32[]{:S(2)}, u32[]{:S(2)}) collective-permute-start(bf16[2,128,512]{2,1,0:T(8,128)(2,1)S(1)} %collective-permute-done.7.refs_5_), channel_id=1, source_target_pairs={{0,14},{2,0},{4,2},{6,4},{8,6},{10,8},{12,10},{14,12},{1,15},{3,1}... | collective-permute-start | bytes 786440 | tf_op jit(solution)/shard_map/ppermute | solution.py:75
  51.8 3.5 %collective-permute-done.4.refs_2_ = bf16[2,128,512]{2,1,0:T(8,128)(2,1)S(1)} collective-permute-done((bf16[2,128,512]{2,1,0:T(8,128)(2,1)S(1)}, bf16[2,128,512]{2,1,0:T(8,128)(2,1)S(1)}, u32[]{:S(2)}, u32[]{:S(2)}) %collective-permute-start.4) | collective-permute-done | bytes 262176 | tf_op jit(solution)/shard_map/ppermute | solution.py:74
  55.4 1.9 %collective-permute-start.5 = (bf16[2,128,512]{2,1,0:T(8,128)(2,1)S(1)}, bf16[2,128,512]{2,1,0:T(8,128)(2,1)S(1)}, u32[]{:S(2)}, u32[]{:S(2)}) collective-permute-start(bf16[2,128,512]{2,1,0:T(8,128)(2,1)S(1)} %collective-permute-done.4.refs_2_), channel_id=1, source_target_pairs={{0,2},{2,4},{4,6},{6,8},{8,10},{10,12},{12,14},{14,0},{1,3},{3,5},... | collective-permute-start | bytes 786440 | tf_op jit(solution)/shard_map/ppermute | solution.py:74
  57.3 5.1 %collective-permute-start.9 = (bf16[2,128,512]{2,1,0:T(8,128)(2,1)S(1)}, bf16[2,128,512]{2,1,0:T(8,128)(2,1)S(1)}, u32[]{:S(2)}, u32[]{:S(2)}) collective-permute-start(bf16[2,128,512]{2,1,0:T(8,128)(2,1)S(1)} %collective-permute-done.8.refs_6_), channel_id=1, source_target_pairs={{0,14},{2,0},{4,2},{6,4},{8,6},{10,8},{12,10},{14,12},{1,15},{3,1}... | collective-permute-start | bytes 786440 | tf_op jit(solution)/shard_map/ppermute | solution.py:75
  62.4 2.6 %collective-permute-done.5.after_right.refs_3_ = bf16[2,128,512]{2,1,0:T(8,128)(2,1)S(1)} collective-permute-done((bf16[2,128,512]{2,1,0:T(8,128)(2,1)S(1)}, bf16[2,128,512]{2,1,0:T(8,128)(2,1)S(1)}, u32[]{:S(2)}, u32[]{:S(2)}) %collective-permute-start.5) | collective-permute-done | bytes 262176 | tf_op jit(solution)/shard_map/ppermute | solution.py:74
  65.1 1.9 %collective-permute-start.6 = (bf16[2,128,512]{2,1,0:T(8,128)(2,1)S(1)}, bf16[2,128,512]{2,1,0:T(8,128)(2,1)}, u32[]{:S(2)}, u32[]{:S(2)}) collective-permute-start(bf16[2,128,512]{2,1,0:T(8,128)(2,1)S(1)} %collective-permute-done.5.after_right.refs_3_), channel_id=1, source_target_pairs={{0,2},{2,4},{4,6},{6,8},{8,10},{10,12},{12,14},{14,0},{1,3},{3,5},... | collective-permute-start | bytes 786440 | tf_op jit(solution)/shard_map/ppermute | solution.py:76
  67.3 0.8 all_to_all.10
  68.1 14.7 %all-to-all-start.1 = ((bf16[64,4,512]{2,1,0:T(4,128)(2,1)}), bf16[64,4,512]{2,1,0:T(4,128)(2,1)S(1)}, u32[]{:S(2)}, u32[]{:S(2)}) async-start(bf16[64,4,512]{2,1,0:T(4,128)(2,1)} %all_to_all.10), calls=%async_computation.1 | async-start | bytes 524288 | tf_op jit(solution)/shard_map/all_to_all | solution.py:330
  82.8 0.6 pad_add_fusion.place
  83.5 7.4 %forward.1 = (f32[192,512]{1,0:T(8,128)}, bf16[192,2048]{1,0:T(8,128)(2,1)}, f32[192,512]{1,0:T(8,128)}, bf16[192,2048]{1,0:T(8,128)(2,1)}) custom-call(s32[2]{0:T(128)} %pad_add_fusion.place, bf16[192,4096]{1,0:T(8,128)(2,1)} %own.3, bf16[192,4096]{1,0:T(8,128)(2,1)} %copy-done.1, bf16[192,512]{1,0:T(8,128)(2,1)} %kg_own.3, bf16[192,512]{1,0:T(8,128)(2,1)} %copy-done.8, ...), custom_call_target="tpu_custom_call" | custom-call | tf_op jit(solution)/shard_map/forward/pallas_call | solution.py:244
  90.9 1.9 %collective-permute-start.11 = (bf16[192,2048]{1,0:T(8,128)(2,1)}, bf16[192,2048]{1,0:T(8,128)(2,1)S(1)}, u32[]{:S(2)}, u32[]{:S(2)}) collective-permute-start(bf16[192,2048]{1,0:T(8,128)(2,1)} %get-tuple-element.16), channel_id=1, source_target_pairs={{0,1},{1,0},{2,3},{3,2},{4,5},{5,4},{6,7},{7,6},{8,9},{9,8},{10,11... | collective-permute-start | bytes 2359304 | tf_op jit(solution)/shard_map/ppermute | solution.py:339
  92.9 2.4 %collective-permute-start.10 = (f32[192,512]{1,0:T(8,128)}, f32[192,512]{1,0:T(8,128)S(1)}, u32[]{:S(2)}, u32[]{:S(2)}) collective-permute-start(f32[192,512]{1,0:T(8,128)} %get-tuple-element.15), channel_id=1, source_target_pairs={{0,1},{1,0},{2,3},{3,2},{4,5},{5,4},{6,7},{7,6},{8,9},{9,8},{10,11... | collective-permute-start | bytes 1179656 | tf_op jit(solution)/shard_map/ppermute | solution.py:338
  95.3 1.5 %collective-permute-done.10.p_other = f32[192,512]{1,0:T(8,128)S(1)} collective-permute-done((f32[192,512]{1,0:T(8,128)}, f32[192,512]{1,0:T(8,128)S(1)}, u32[]{:S(2)}, u32[]{:S(2)}) %collective-permute-start.10) | collective-permute-done | bytes 393248 | tf_op jit(solution)/shard_map/ppermute | solution.py:338
  96.8 0.7 copy-done.13
  97.9 3.7 %finish.1 = (bf16[192,512]{1,0:T(8,128)(2,1)}, bf16[192,4096]{1,0:T(8,128)(2,1)}) custom-call(s32[1]{0:T(128)} %bitcast.core, f32[192,512]{1,0:T(8,128)} %get-tuple-element.13.p_own, bf16[192,2048]{1,0:T(8,128)(2,1)} %get-tuple-element.14.t_own, f32[192,512]{1,0:T(8,128)} %copy-done.13, bf16[192,2048]{1,0:T(8,128)(2,1)} %copy-done.12, f32[384,128]{1,0:T(8,128)} %copy-done.3, ...), custom_call_target="tpu_custom_call" | custom-call | tf_op jit(solution)/shard_map/finish/pallas_call | solution.py:290
  101.6 2.7 %all-to-all-done.1 = bf16[64,4,512]{2,1,0:T(4,128)(2,1)S(1)} async-done(((bf16[64,4,512]{2,1,0:T(4,128)(2,1)}), bf16[64,4,512]{2,1,0:T(4,128)(2,1)S(1)}, u32[]{:S(2)}, u32[]{:S(2)}) %all-to-all-start.1) | async-done | bytes 262176 | tf_op jit(solution)/shard_map/all_to_all | solution.py:330
  104.4 0.6 multiply_convert_fusion
  (46 shorter events, 1.0 us)
Async XLA Ops:
  0.6 10.6 %collective-permute-start = (bf16[192,4096]{1,0:T(8,128)(2,1)}, bf16[192,4096]{1,0:T(8,128)(2,1)S(1)}, u32[]{:S(2)}, u32[]{:S(2)}) collective-permute-start(bf16[192,4096]{1,0:T(8,128)(2,1)} %own.3), channel_id=1, source_target_pairs={{0,1},{1,0},{2,3},{3,2},{4,5},{5,4},{6,7},{7,6},{8,9},{9,8},{10,11... | collective-permute-start | bytes 4718600 | tf_op jit(solution)/shard_map/ppermute | solution.py:316
  2.6 0.9 copy-start.10
  3.5 0.7 copy-start.11
  4.2 12.8 %collective-permute-start.2 = (bf16[128,512]{1,0:T(8,128)(2,1)S(1)}, bf16[128,512]{1,0:T(8,128)(2,1)S(1)}, u32[]{:S(2)}, u32[]{:S(2)}) collective-permute-start(bf16[128,512]{1,0:T(8,128)(2,1)S(1)} %dequantize.1.own), channel_id=1, source_target_pairs={{0,528},{16,512},{512,16},{528,0},{1,529},{17,513},{513,17},{529,1... | collective-permute-start | bytes 393224 | tf_op jit(solution)/shard_map/ppermute | solution.py:315
  7.6 3.5 %collective-permute-start.1 = (bf16[192,512]{1,0:T(8,128)(2,1)}, bf16[192,512]{1,0:T(8,128)(2,1)S(1)}, u32[]{:S(2)}, u32[]{:S(2)}) collective-permute-start(bf16[192,512]{1,0:T(8,128)(2,1)} %kg_own.3), channel_id=1, source_target_pairs={{0,1},{1,0},{2,3},{3,2},{4,5},{5,4},{6,7},{7,6},{8,9},{9,8},{10,11... | collective-permute-start | bytes 589832 | tf_op jit(solution)/shard_map/ppermute | solution.py:317
  10.7 6.3 %copy-start.2 = (f32[384,128]{1,0:T(8,128)}, f32[384,128]{1,0:T(8,128)S(1)}, u32[]{:S(2)}) copy-start(f32[384,128]{1,0:T(8,128)S(1)} %get-tuple-element.19.sin) | copy-start | bytes 589828
  10.7 6.3 %copy-start.3 = (f32[384,128]{1,0:T(8,128)}, f32[384,128]{1,0:T(8,128)S(1)}, u32[]{:S(2)}) copy-start(f32[384,128]{1,0:T(8,128)S(1)} %get-tuple-element.20.cos) | copy-start | bytes 589828
  11.2 5.8 %copy-start.8 = (bf16[192,512]{1,0:T(8,128)(2,1)}, bf16[192,512]{1,0:T(8,128)(2,1)S(1)}, u32[]{:S(2)}) copy-start(bf16[192,512]{1,0:T(8,128)(2,1)S(1)} %collective-permute-done.1.kg_other) | copy-start | bytes 589828
  11.2 5.8 %copy-start.1 = (bf16[192,4096]{1,0:T(8,128)(2,1)}, bf16[192,4096]{1,0:T(8,128)(2,1)S(1)}, u32[]{:S(2)}) copy-start(bf16[192,4096]{1,0:T(8,128)(2,1)S(1)} %collective-permute-done.other) | copy-start | bytes 4718596
  11.2 2.0 %copy-start = (bf16[192,4096]{1,0:T(8,128)(2,1)S(1)}, bf16[192,4096]{1,0:T(8,128)(2,1)}, u32[]{:S(2)}) copy-start(bf16[192,4096]{1,0:T(8,128)(2,1)} %own.3) | copy-start | bytes 4718596
  13.2 0.9 copy-start.7
  17.0 18.2 %copy-start.9 = (bf16[2,128,512]{2,1,0:T(8,128)(2,1)}, bf16[2,128,512]{2,1,0:T(8,128)(2,1)S(1)}, u32[]{:S(2)}) copy-start(bf16[2,128,512]{2,1,0:T(8,128)(2,1)S(1)} %get-tuple-element.11.refs_0_) | copy-start | bytes 786436
  17.0 50.0 %all-to-all-start = ((bf16[16,256,256]{2,1,0:T(8,128)(2,1)}), bf16[16,256,256]{2,1,0:T(8,128)(2,1)S(1)}, u32[]{:S(2)}, u32[]{:S(2)}) async-start(bf16[16,256,256]{2,1,0:T(8,128)(2,1)} %bitcast.4), calls=%async_computation | async-start | bytes 4194304 | tf_op jit(solution)/shard_map/all_to_all | solution.py:328
  33.3 11.5 %collective-permute-start.3 = (bf16[2,128,512]{2,1,0:T(8,128)(2,1)S(1)}, bf16[2,128,512]{2,1,0:T(8,128)(2,1)S(1)}, u32[]{:S(2)}, u32[]{:S(2)}) collective-permute-start(bf16[2,128,512]{2,1,0:T(8,128)(2,1)S(1)} %get-tuple-element.11.refs_0_), channel_id=1, source_target_pairs={{0,2},{2,4},{4,6},{6,8},{8,10},{10,12},{12,14},{14,0},{1,3},{3,5},... | collective-permute-start | bytes 786440 | tf_op jit(solution)/shard_map/ppermute | solution.py:74
  35.2 11.4 %collective-permute-start.7 = (bf16[2,128,512]{2,1,0:T(8,128)(2,1)S(1)}, bf16[2,128,512]{2,1,0:T(8,128)(2,1)S(1)}, u32[]{:S(2)}, u32[]{:S(2)}) collective-permute-start(bf16[2,128,512]{2,1,0:T(8,128)(2,1)S(1)} %get-tuple-element.11.refs_0_), channel_id=1, source_target_pairs={{0,14},{2,0},{4,2},{6,4},{8,6},{10,8},{12,10},{14,12},{1,15},{3,1}... | collective-permute-start | bytes 786440 | tf_op jit(solution)/shard_map/ppermute | solution.py:75
  44.7 38.7 %copy-start.14 = (bf16[2,128,512]{2,1,0:T(8,128)(2,1)}, bf16[2,128,512]{2,1,0:T(8,128)(2,1)S(1)}, u32[]{:S(2)}) copy-start(bf16[2,128,512]{2,1,0:T(8,128)(2,1)S(1)} %collective-permute-done.3.refs_1_) | copy-start | bytes 786436
  44.7 10.6 %collective-permute-start.4 = (bf16[2,128,512]{2,1,0:T(8,128)(2,1)S(1)}, bf16[2,128,512]{2,1,0:T(8,128)(2,1)S(1)}, u32[]{:S(2)}, u32[]{:S(2)}) collective-permute-start(bf16[2,128,512]{2,1,0:T(8,128)(2,1)S(1)} %collective-permute-done.3.refs_1_), channel_id=1, source_target_pairs={{0,2},{2,4},{4,6},{6,8},{8,10},{10,12},{12,14},{14,0},{1,3},{3,5},... | collective-permute-start | bytes 786440 | tf_op jit(solution)/shard_map/ppermute | solution.py:74
  46.7 20.4 %copy-start.15 = (bf16[2,128,512]{2,1,0:T(8,128)(2,1)}, bf16[2,128,512]{2,1,0:T(8,128)(2,1)S(1)}, u32[]{:S(2)}) copy-start(bf16[2,128,512]{2,1,0:T(8,128)(2,1)S(1)} %collective-permute-done.7.refs_5_) | copy-start | bytes 786436
  46.7 10.6 %collective-permute-start.8 = (bf16[2,128,512]{2,1,0:T(8,128)(2,1)S(1)}, bf16[2,128,512]{2,1,0:T(8,128)(2,1)S(1)}, u32[]{:S(2)}, u32[]{:S(2)}) collective-permute-start(bf16[2,128,512]{2,1,0:T(8,128)(2,1)S(1)} %collective-permute-done.7.refs_5_), channel_id=1, source_target_pairs={{0,14},{2,0},{4,2},{6,4},{8,6},{10,8},{12,10},{14,12},{1,15},{3,1}... | collective-permute-start | bytes 786440 | tf_op jit(solution)/shard_map/ppermute | solution.py:75
  55.4 11.6 %copy-start.16 = (bf16[2,128,512]{2,1,0:T(8,128)(2,1)}, bf16[2,128,512]{2,1,0:T(8,128)(2,1)S(1)}, u32[]{:S(2)}) copy-start(bf16[2,128,512]{2,1,0:T(8,128)(2,1)S(1)} %collective-permute-done.4.refs_2_) | copy-start | bytes 786436
  55.4 9.7 %collective-permute-start.5 = (bf16[2,128,512]{2,1,0:T(8,128)(2,1)S(1)}, bf16[2,128,512]{2,1,0:T(8,128)(2,1)S(1)}, u32[]{:S(2)}, u32[]{:S(2)}) collective-permute-start(bf16[2,128,512]{2,1,0:T(8,128)(2,1)S(1)} %collective-permute-done.4.refs_2_), channel_id=1, source_target_pairs={{0,2},{2,4},{4,6},{6,8},{8,10},{10,12},{12,14},{14,0},{1,3},{3,5},... | collective-permute-start | bytes 786440 | tf_op jit(solution)/shard_map/ppermute | solution.py:74
  57.3 26.2 %copy-start.17 = (bf16[2,128,512]{2,1,0:T(8,128)(2,1)}, bf16[2,128,512]{2,1,0:T(8,128)(2,1)S(1)}, u32[]{:S(2)}) copy-start(bf16[2,128,512]{2,1,0:T(8,128)(2,1)S(1)} %collective-permute-done.8.refs_6_) | copy-start | bytes 786436
  57.3 9.7 %collective-permute-start.9 = (bf16[2,128,512]{2,1,0:T(8,128)(2,1)S(1)}, bf16[2,128,512]{2,1,0:T(8,128)(2,1)S(1)}, u32[]{:S(2)}, u32[]{:S(2)}) collective-permute-start(bf16[2,128,512]{2,1,0:T(8,128)(2,1)S(1)} %collective-permute-done.8.refs_6_), channel_id=1, source_target_pairs={{0,14},{2,0},{4,2},{6,4},{8,6},{10,8},{12,10},{14,12},{1,15},{3,1}... | collective-permute-start | bytes 786440 | tf_op jit(solution)/shard_map/ppermute | solution.py:75
  65.1 18.4 %copy-start.5 = (bf16[2,128,512]{2,1,0:T(8,128)(2,1)}, bf16[2,128,512]{2,1,0:T(8,128)(2,1)S(1)}, u32[]{:S(2)}) copy-start(bf16[2,128,512]{2,1,0:T(8,128)(2,1)S(1)} %collective-permute-done.5.after_right.refs_3_) | copy-start | bytes 786436
  65.1 18.4 %collective-permute-start.6 = (bf16[2,128,512]{2,1,0:T(8,128)(2,1)S(1)}, bf16[2,128,512]{2,1,0:T(8,128)(2,1)}, u32[]{:S(2)}, u32[]{:S(2)}) collective-permute-start(bf16[2,128,512]{2,1,0:T(8,128)(2,1)S(1)} %collective-permute-done.5.after_right.refs_3_), channel_id=1, source_target_pairs={{0,2},{2,4},{4,6},{6,8},{8,10},{10,12},{12,14},{14,0},{1,3},{3,5},... | collective-permute-start | bytes 786440 | tf_op jit(solution)/shard_map/ppermute | solution.py:76
  67.0 16.5 %copy-start.6 = (bf16[2,128,512]{2,1,0:T(8,128)(2,1)}, bf16[2,128,512]{2,1,0:T(8,128)(2,1)S(1)}, u32[]{:S(2)}) copy-start(bf16[2,128,512]{2,1,0:T(8,128)(2,1)S(1)} %collective-permute-done.9.after_left.refs_7_) | copy-start | bytes 786436
  67.3 16.2 %copy-start.4 = (bf16[256,512]{1,0:T(8,128)(2,1)}, bf16[256,512]{1,0:T(8,128)(2,1)S(1)}, u32[]{:S(2)}) copy-start(bf16[256,512]{1,0:T(8,128)(2,1)S(1)} %near_total.1.refs_8_) | copy-start | bytes 786436
  68.1 36.2 %all-to-all-start.1 = ((bf16[64,4,512]{2,1,0:T(4,128)(2,1)}), bf16[64,4,512]{2,1,0:T(4,128)(2,1)S(1)}, u32[]{:S(2)}, u32[]{:S(2)}) async-start(bf16[64,4,512]{2,1,0:T(4,128)(2,1)} %all_to_all.10), calls=%async_computation.1 | async-start | bytes 524288 | tf_op jit(solution)/shard_map/all_to_all | solution.py:330
  90.9 5.9 %collective-permute-start.11 = (bf16[192,2048]{1,0:T(8,128)(2,1)}, bf16[192,2048]{1,0:T(8,128)(2,1)S(1)}, u32[]{:S(2)}, u32[]{:S(2)}) collective-permute-start(bf16[192,2048]{1,0:T(8,128)(2,1)} %get-tuple-element.16), channel_id=1, source_target_pairs={{0,1},{1,0},{2,3},{3,2},{4,5},{5,4},{6,7},{7,6},{8,9},{9,8},{10,11... | collective-permute-start | bytes 2359304 | tf_op jit(solution)/shard_map/ppermute | solution.py:339
  92.9 4.0 %collective-permute-start.10 = (f32[192,512]{1,0:T(8,128)}, f32[192,512]{1,0:T(8,128)S(1)}, u32[]{:S(2)}, u32[]{:S(2)}) collective-permute-start(f32[192,512]{1,0:T(8,128)} %get-tuple-element.15), channel_id=1, source_target_pairs={{0,1},{1,0},{2,3},{3,2},{4,5},{5,4},{6,7},{7,6},{8,9},{9,8},{10,11... | collective-permute-start | bytes 1179656 | tf_op jit(solution)/shard_map/ppermute | solution.py:338
  96.8 0.7 copy-start.13
  96.8 1.0 copy-start.12

commit v4 on v3

--- a/solution.py
+++ b/solution.py
@@ -170,11 +170,11 @@
     )(core, own, other, kg_own, kg_other, cos, sin)
 
 
-def forward_kernel(place, own, other, kg_own, kg_other, cos, sin, *refs):
+def forward_kernel(core_ref, y_ref, own, other, kg_own, kg_other, cos, sin, *refs):
     blocks, (after, p_out, t_out, p_sent, t_sent) = refs[:8], refs[8:13]
     t_own, t_other, held, kg, weights, proj_grad, total, sems = refs[13:]
     rows, kvw = kg_own.shape
-    core, y = place[0], place[1]
+    core, y = core_ref[0], y_ref[0]
     part = rows // 4
     pairs = [(kg_own, kg.at[pl.ds(0, rows)]), (kg_other, kg.at[pl.ds(rows, rows)])]
     pairs += [(block, weights.at[k]) for k, block in enumerate(blocks)]
@@ -236,7 +236,7 @@
         copy.wait()
 
 
-def forward(place, own, other, kg_own, kg_other, cos, sin, blocks, after):
+def forward(core, y, own, other, kg_own, kg_other, cos, sin, blocks, after):
     rows, features = own.shape
     kvw = kg_own.shape[1]
     vmem = pl.BlockSpec(memory_space=pltpu.VMEM)
@@ -249,7 +249,7 @@
             jax.ShapeDtypeStruct((rows, kvw), jnp.float32),
             jax.ShapeDtypeStruct((rows, features // 2), jnp.bfloat16),
         ),
-        in_specs=[pl.BlockSpec(memory_space=pltpu.SMEM)]
+        in_specs=[pl.BlockSpec(memory_space=pltpu.SMEM)] * 2
         + [anywhere] * 4
         + [vmem] * 2
         + [anywhere] * 9,
@@ -267,7 +267,7 @@
         compiler_params=pltpu.CompilerParams(vmem_limit_bytes=WIDE),
         cost_estimate=QUICK,
         name="forward",
-    )(place, own, other, kg_own, kg_other, cos, sin, *blocks, after)
+    )(core, y, own, other, kg_own, kg_other, cos, sin, *blocks, after)
 
 
 def finish_kernel(core, p_own, t_own, p_other, t_other, cos, sin, rotated, token_grad):
@@ -298,7 +298,7 @@
         + [block(kvw), block(features // 2)] * 2
         + [block(HEAD_DIM)] * 2,
         out_specs=(block(kvw), block(features)),
-        compiler_params=pltpu.CompilerParams(vmem_limit_bytes=WIDE),
+        compiler_params=pltpu.CompilerParams(vmem_limit_bytes=GRANT),
         cost_estimate=QUICK,
         name="finish",
     )(core, p_own, t_own, p_other, t_other, cos, sin)
@@ -328,17 +328,19 @@
     near = lax.all_to_all(partial.reshape(16, 256, kvw // 2), NEAR, 0, 0)
     near_sum = near_total(near.reshape(8, 2, 256, kvw // 2), blocks[3], blocks[7])
     far = lax.all_to_all(near_sum, FAR, 0, 0, tiled=True)
-    summed = far.reshape(64, 4, kvw).astype(jnp.float32).sum(0)
-    count = rows * math.prod(SIZES.values())
-
-    where = jnp.stack([core, lax.axis_index(("yh", "yl"))])
     p_own, t_own, p_sent, t_sent = forward(
-        where, tokens, other_tokens, key_grad, other_key_grad, cos, sin, blocks, near_sum
+        core.reshape(1),
+        lax.axis_index(("yh", "yl")).reshape(1),
+        tokens,
+        other_tokens,
+        key_grad, other_key_grad, cos, sin, blocks, near_sum
     )
     p_other = lax.ppermute(p_sent, "c", SWAP)
     t_other = lax.ppermute(t_sent, "c", SWAP)
     rotated, token_grad = finish(core.reshape(1), p_own, t_own, p_other, t_other, cos, sin)
-    weight_grad = (summed * (1.0 / math.sqrt(count))).astype(jnp.bfloat16)
+    count = rows * math.prod(SIZES.values())
+    scaled = far.reshape(64, 4, kvw).astype(jnp.float32) * (1.0 / math.sqrt(count))
+    weight_grad = scaled.sum(0).astype(jnp.bfloat16)
     return (rotated, token_grad, weight_grad)
 
 

time: 106 us -> 106 us (level)
  Pallas kernels: 14.4 us -> 12.5 us
  waiting for transfers between devices: 15.3 us -> 16.6 us
  local copies, waits for them, and re-layouts: 6.41 us -> 7.53 us
    pallas_call x1, Pallas kernels: 3.72 us -> 1.85 us  [finish(): pl.pallas_call(finish_kernel, grid=(steps,), out_shape=(jax.ShapeDtypeStr...]
    all_to_all x1, waiting for transfers between devices: 2.72 us -> 4.02 us  [body(): far = lax.all_to_all(near_sum, FAR, 0, 0, tiled=True)]
    unnamed x36 -> x40, local copies, waits for them, and re-layouts: 5.62 us -> 6.7 us
  transfers between devices with their start and end apart: 14 -> 14, of which waited for: 6 -> 6; matrix products, arithmetic and copies ran while one was open for 1% -> 1% of each run, Pallas kernels for 14% -> 12%
where the time goes in v4:
time: 106 us; the launch traced here: 105 us
  starting transfers between devices  65.7 us (62%)
  waiting for transfers between devices  16.6 us (16%)
  Pallas kernels  12.5 us (12%)
  local copies, waits for them, and re-layouts  7.53 us (7%)
  other arithmetic  1.62 us (2%)
    all_to_all x1, starting transfers between devices, body(): near = lax.all_to_all(partial.reshape(16, 256, kvw // 2), NEAR, 0, 0)  16.2 us
    ppermute x3, starting transfers between devices, gather(): lefts.append(lax.ppermute(lefts[-1], axes, left))  15.4 us
    all_to_all x1, starting transfers between devices, body(): far = lax.all_to_all(near_sum, FAR, 0, 0, tiled=True)  14.7 us
    ppermute x4, waiting for transfers between devices, gather(): rights.append(lax.ppermute(rights[-1], axes, right))  10.6 us
    ppermute x4, starting transfers between devices, gather(): rights.append(lax.ppermute(rights[-1], axes, right))  7.64 us
    pallas_call x1, Pallas kernels, forward(): pl.pallas_call(forward_kernel, out_shape=(jax.ShapeDtypeStruct((rows, kvw...  7.47 us
    unnamed x40, local copies, waits for them, and re-layouts  6.7 us
    all_to_all x1, waiting for transfers between devices, body(): far = lax.all_to_all(near_sum, FAR, 0, 0, tiled=True)  4.02 us
  transfers between devices with their start and end apart: 14, of which 6 were waited for; matrix products, arithmetic and copies ran while one was open for 1% of the time, Pallas kernels for 12%

profile of v4, /device:TPU:2, one launch (start us, length us, event | category | flops | bytes accessed | tf_op | source)
XLA Modules:
  0.0 105.1 jit_solution(4878006774241142713)
XLA Ops:
  0.6 1.9 %collective-permute-start = (bf16[192,4096]{1,0:T(8,128)(2,1)}, bf16[192,4096]{1,0:T(8,128)(2,1)S(1)}, u32[]{:S(2)}, u32[]{:S(2)}) collective-permute-start(bf16[192,4096]{1,0:T(8,128)(2,1)} %own.3), channel_id=1, source_target_pairs={{0,1},{1,0},{2,3},{3,2},{4,5},{5,4},{6,7},{7,6},{8,9},{9,8},{10,11... | collective-permute-start | bytes 4718600 | tf_op jit(solution)/shard_map/ppermute | solution.py:316
  2.6 0.9 copy-done.14
  3.5 0.7 copy-done.15
  4.2 3.4 %collective-permute-start.2 = (bf16[128,512]{1,0:T(8,128)(2,1)S(1)}, bf16[128,512]{1,0:T(8,128)(2,1)S(1)}, u32[]{:S(2)}, u32[]{:S(2)}) collective-permute-start(bf16[128,512]{1,0:T(8,128)(2,1)S(1)} %dequantize.1.own), channel_id=1, source_target_pairs={{0,528},{16,512},{512,16},{528,0},{1,529},{17,513},{513,17},{529,1... | collective-permute-start | bytes 393224 | tf_op jit(solution)/shard_map/ppermute | solution.py:315
  7.6 2.1 %collective-permute-start.1 = (bf16[192,512]{1,0:T(8,128)(2,1)}, bf16[192,512]{1,0:T(8,128)(2,1)S(1)}, u32[]{:S(2)}, u32[]{:S(2)}) collective-permute-start(bf16[192,512]{1,0:T(8,128)(2,1)} %kg_own.3), channel_id=1, source_target_pairs={{0,1},{1,0},{2,3},{3,2},{4,5},{5,4},{6,7},{7,6},{8,9},{9,8},{10,11... | collective-permute-start | bytes 589832 | tf_op jit(solution)/shard_map/ppermute | solution.py:317
  9.9 0.8 fusion
  10.7 0.5 collective-permute-done.1.kg_other
  11.2 2.0 %copy-done = bf16[192,4096]{1,0:T(8,128)(2,1)S(1)} copy-done((bf16[192,4096]{1,0:T(8,128)(2,1)S(1)}, bf16[192,4096]{1,0:T(8,128)(2,1)}, u32[]{:S(2)}) %copy-start) | copy-done | bytes 1572888
  13.2 0.9 copy-done.9
  14.2 2.8 %weight_partial.1.passed = bf16[2,4,2,8,32,256]{5,4,3,2,1,0:T(8,128)(2,1)} custom-call(s32[1]{0:T(128)} %bitcast.core.core_ref, bf16[192,4096]{1,0:T(8,128)(2,1)S(1)} %copy-done, bf16[192,4096]{1,0:T(8,128)(2,1)S(1)} %collective-permute-done.other, bf16[192,512]{1,0:T(8,128)(2,1)S(1)} %copy-done.9, bf16[192,512]{1,0:T(8,128)(2,1)S(1)} %collective-permute-done.1.kg_other, ...), custom_call_target="tpu_custom_call" | custom-call | flops 805306368 | bytes 8388608 | tf_op jit(solution)/shard_map/weight_partial/pallas_call | solution.py:159
  17.1 16.2 %all-to-all-start = ((bf16[16,256,256]{2,1,0:T(8,128)(2,1)}), bf16[16,256,256]{2,1,0:T(8,128)(2,1)S(1)}, u32[]{:S(2)}, u32[]{:S(2)}) async-start(bf16[16,256,256]{2,1,0:T(8,128)(2,1)} %bitcast.4), calls=%async_computation | async-start | bytes 4194304 | tf_op jit(solution)/shard_map/all_to_all | solution.py:328
  33.3 1.9 %collective-permute-start.3 = (bf16[2,128,512]{2,1,0:T(8,128)(2,1)S(1)}, bf16[2,128,512]{2,1,0:T(8,128)(2,1)S(1)}, u32[]{:S(2)}, u32[]{:S(2)}) collective-permute-start(bf16[2,128,512]{2,1,0:T(8,128)(2,1)S(1)} %get-tuple-element.11.refs_0_), channel_id=1, source_target_pairs={{0,2},{2,4},{4,6},{6,8},{8,10},{10,12},{12,14},{14,0},{1,3},{3,5},... | collective-permute-start | bytes 786440 | tf_op jit(solution)/shard_map/ppermute | solution.py:74
  35.2 5.1 %collective-permute-start.7 = (bf16[2,128,512]{2,1,0:T(8,128)(2,1)S(1)}, bf16[2,128,512]{2,1,0:T(8,128)(2,1)S(1)}, u32[]{:S(2)}, u32[]{:S(2)}) collective-permute-start(bf16[2,128,512]{2,1,0:T(8,128)(2,1)S(1)} %get-tuple-element.11.refs_0_), channel_id=1, source_target_pairs={{0,14},{2,0},{4,2},{6,4},{8,6},{10,8},{12,10},{14,12},{1,15},{3,1}... | collective-permute-start | bytes 786440 | tf_op jit(solution)/shard_map/ppermute | solution.py:75
  40.4 4.4 %collective-permute-done.3.refs_1_ = bf16[2,128,512]{2,1,0:T(8,128)(2,1)S(1)} collective-permute-done((bf16[2,128,512]{2,1,0:T(8,128)(2,1)S(1)}, bf16[2,128,512]{2,1,0:T(8,128)(2,1)S(1)}, u32[]{:S(2)}, u32[]{:S(2)}) %collective-permute-start.3) | collective-permute-done | bytes 262176 | tf_op jit(solution)/shard_map/ppermute | solution.py:74
  44.7 1.9 %collective-permute-start.4 = (bf16[2,128,512]{2,1,0:T(8,128)(2,1)S(1)}, bf16[2,128,512]{2,1,0:T(8,128)(2,1)S(1)}, u32[]{:S(2)}, u32[]{:S(2)}) collective-permute-start(bf16[2,128,512]{2,1,0:T(8,128)(2,1)S(1)} %collective-permute-done.3.refs_1_), channel_id=1, source_target_pairs={{0,2},{2,4},{4,6},{6,8},{8,10},{10,12},{12,14},{14,0},{1,3},{3,5},... | collective-permute-start | bytes 786440 | tf_op jit(solution)/shard_map/ppermute | solution.py:74
  46.7 5.1 %collective-permute-start.8 = (bf16[2,128,512]{2,1,0:T(8,128)(2,1)S(1)}, bf16[2,128,512]{2,1,0:T(8,128)(2,1)S(1)}, u32[]{:S(2)}, u32[]{:S(2)}) collective-permute-start(bf16[2,128,512]{2,1,0:T(8,128)(2,1)S(1)} %collective-permute-done.7.refs_5_), channel_id=1, source_target_pairs={{0,14},{2,0},{4,2},{6,4},{8,6},{10,8},{12,10},{14,12},{1,15},{3,1}... | collective-permute-start | bytes 786440 | tf_op jit(solution)/shard_map/ppermute | solution.py:75
  51.8 3.5 %collective-permute-done.4.refs_2_ = bf16[2,128,512]{2,1,0:T(8,128)(2,1)S(1)} collective-permute-done((bf16[2,128,512]{2,1,0:T(8,128)(2,1)S(1)}, bf16[2,128,512]{2,1,0:T(8,128)(2,1)S(1)}, u32[]{:S(2)}, u32[]{:S(2)}) %collective-permute-start.4) | collective-permute-done | bytes 262176 | tf_op jit(solution)/shard_map/ppermute | solution.py:74
  55.4 1.9 %collective-permute-start.5 = (bf16[2,128,512]{2,1,0:T(8,128)(2,1)S(1)}, bf16[2,128,512]{2,1,0:T(8,128)(2,1)S(1)}, u32[]{:S(2)}, u32[]{:S(2)}) collective-permute-start(bf16[2,128,512]{2,1,0:T(8,128)(2,1)S(1)} %collective-permute-done.4.refs_2_), channel_id=1, source_target_pairs={{0,2},{2,4},{4,6},{6,8},{8,10},{10,12},{12,14},{14,0},{1,3},{3,5},... | collective-permute-start | bytes 786440 | tf_op jit(solution)/shard_map/ppermute | solution.py:74
  57.3 5.1 %collective-permute-start.9 = (bf16[2,128,512]{2,1,0:T(8,128)(2,1)S(1)}, bf16[2,128,512]{2,1,0:T(8,128)(2,1)S(1)}, u32[]{:S(2)}, u32[]{:S(2)}) collective-permute-start(bf16[2,128,512]{2,1,0:T(8,128)(2,1)S(1)} %collective-permute-done.8.refs_6_), channel_id=1, source_target_pairs={{0,14},{2,0},{4,2},{6,4},{8,6},{10,8},{12,10},{14,12},{1,15},{3,1}... | collective-permute-start | bytes 786440 | tf_op jit(solution)/shard_map/ppermute | solution.py:75
  62.4 2.6 %collective-permute-done.5.after_right.refs_3_ = bf16[2,128,512]{2,1,0:T(8,128)(2,1)S(1)} collective-permute-done((bf16[2,128,512]{2,1,0:T(8,128)(2,1)S(1)}, bf16[2,128,512]{2,1,0:T(8,128)(2,1)S(1)}, u32[]{:S(2)}, u32[]{:S(2)}) %collective-permute-start.5) | collective-permute-done | bytes 262176 | tf_op jit(solution)/shard_map/ppermute | solution.py:74
  65.1 1.9 %collective-permute-start.6 = (bf16[2,128,512]{2,1,0:T(8,128)(2,1)S(1)}, bf16[2,128,512]{2,1,0:T(8,128)(2,1)}, u32[]{:S(2)}, u32[]{:S(2)}) collective-permute-start(bf16[2,128,512]{2,1,0:T(8,128)(2,1)S(1)} %collective-permute-done.5.after_right.refs_3_), channel_id=1, source_target_pairs={{0,2},{2,4},{4,6},{6,8},{8,10},{10,12},{12,14},{14,0},{1,3},{3,5},... | collective-permute-start | bytes 786440 | tf_op jit(solution)/shard_map/ppermute | solution.py:76
  67.3 0.8 all_to_all.10
  68.2 14.7 %all-to-all-start.1 = ((bf16[64,4,512]{2,1,0:T(4,128)(2,1)}), bf16[64,4,512]{2,1,0:T(4,128)(2,1)S(1)}, u32[]{:S(2)}, u32[]{:S(2)}) async-start(bf16[64,4,512]{2,1,0:T(4,128)(2,1)} %all_to_all.10), calls=%async_computation.1 | async-start | bytes 524288 | tf_op jit(solution)/shard_map/all_to_all | solution.py:330
  83.0 7.5 %forward.1 = (f32[192,512]{1,0:T(8,128)}, bf16[192,2048]{1,0:T(8,128)(2,1)}, f32[192,512]{1,0:T(8,128)}, bf16[192,2048]{1,0:T(8,128)(2,1)}) custom-call(s32[1]{0:T(128)} %bitcast.core.core_ref, s32[1]{0:T(128)} %bitcast.1.y_ref, bf16[192,4096]{1,0:T(8,128)(2,1)} %own.3, bf16[192,4096]{1,0:T(8,128)(2,1)} %copy-done.1, bf16[192,512]{1,0:T(8,128)(2,1)} %kg_own.3, ...), custom_call_target="tpu_custom_call" | custom-call | tf_op jit(solution)/shard_map/forward/pallas_call | solution.py:244
  90.4 1.9 %collective-permute-start.11 = (bf16[192,2048]{1,0:T(8,128)(2,1)}, bf16[192,2048]{1,0:T(8,128)(2,1)S(1)}, u32[]{:S(2)}, u32[]{:S(2)}) collective-permute-start(bf16[192,2048]{1,0:T(8,128)(2,1)} %get-tuple-element.16), channel_id=1, source_target_pairs={{0,1},{1,0},{2,3},{3,2},{4,5},{5,4},{6,7},{7,6},{8,9},{9,8},{10,11... | collective-permute-start | bytes 2359304 | tf_op jit(solution)/shard_map/ppermute | solution.py:339
  92.4 2.4 %collective-permute-start.10 = (f32[192,512]{1,0:T(8,128)}, f32[192,512]{1,0:T(8,128)S(1)}, u32[]{:S(2)}, u32[]{:S(2)}) collective-permute-start(f32[192,512]{1,0:T(8,128)} %get-tuple-element.15), channel_id=1, source_target_pairs={{0,1},{1,0},{2,3},{3,2},{4,5},{5,4},{6,7},{7,6},{8,9},{9,8},{10,11... | collective-permute-start | bytes 1179656 | tf_op jit(solution)/shard_map/ppermute | solution.py:338
  94.8 1.5 %collective-permute-done.10.p_other = f32[192,512]{1,0:T(8,128)S(1)} collective-permute-done((f32[192,512]{1,0:T(8,128)}, f32[192,512]{1,0:T(8,128)S(1)}, u32[]{:S(2)}, u32[]{:S(2)}) %collective-permute-start.10) | collective-permute-done | bytes 393248 | tf_op jit(solution)/shard_map/ppermute | solution.py:338
  96.3 1.1 %copy-done.11 = bf16[192,2048]{1,0:T(8,128)(2,1)S(1)} copy-done((bf16[192,2048]{1,0:T(8,128)(2,1)S(1)}, bf16[192,2048]{1,0:T(8,128)(2,1)}, u32[]{:S(2)}) %copy-start.11) | copy-done | bytes 786456
  97.5 1.0 copy-done.12
  98.5 1.9 %finish.1 = (bf16[192,512]{1,0:T(8,128)(2,1)}, bf16[192,4096]{1,0:T(8,128)(2,1)}) custom-call(s32[1]{0:T(128)} %bitcast.core.core_ref, f32[192,512]{1,0:T(8,128)S(1)} %copy-done.12, bf16[192,2048]{1,0:T(8,128)(2,1)S(1)} %copy-done.11, f32[192,512]{1,0:T(8,128)S(1)} %collective-permute-done.10.p_other, bf16[192,2048]{1,0:T(8,128)(2,1)S(1)} %collective-permute-done.11.t_other, ...), custom_call_target="tpu_custom_call" | custom-call | tf_op jit(solution)/shard_map/finish/pallas_call | solution.py:290
  100.3 4.0 %all-to-all-done.1 = bf16[64,4,512]{2,1,0:T(4,128)(2,1)S(1)} async-done(((bf16[64,4,512]{2,1,0:T(4,128)(2,1)}), bf16[64,4,512]{2,1,0:T(4,128)(2,1)S(1)}, u32[]{:S(2)}, u32[]{:S(2)}) %all-to-all-start.1) | async-done | bytes 262176 | tf_op jit(solution)/shard_map/all_to_all | solution.py:330
  104.3 0.8 multiply_reduce_fusion
  (48 shorter events, 0.6 us)
Async XLA Ops:
  0.6 10.6 %collective-permute-start = (bf16[192,4096]{1,0:T(8,128)(2,1)}, bf16[192,4096]{1,0:T(8,128)(2,1)S(1)}, u32[]{:S(2)}, u32[]{:S(2)}) collective-permute-start(bf16[192,4096]{1,0:T(8,128)(2,1)} %own.3), channel_id=1, source_target_pairs={{0,1},{1,0},{2,3},{3,2},{4,5},{5,4},{6,7},{7,6},{8,9},{9,8},{10,11... | collective-permute-start | bytes 4718600 | tf_op jit(solution)/shard_map/ppermute | solution.py:316
  4.2 12.8 %collective-permute-start.2 = (bf16[128,512]{1,0:T(8,128)(2,1)S(1)}, bf16[128,512]{1,0:T(8,128)(2,1)S(1)}, u32[]{:S(2)}, u32[]{:S(2)}) collective-permute-start(bf16[128,512]{1,0:T(8,128)(2,1)S(1)} %dequantize.1.own), channel_id=1, source_target_pairs={{0,528},{16,512},{512,16},{528,0},{1,529},{17,513},{513,17},{529,1... | collective-permute-start | bytes 393224 | tf_op jit(solution)/shard_map/ppermute | solution.py:315
  7.6 3.5 %collective-permute-start.1 = (bf16[192,512]{1,0:T(8,128)(2,1)}, bf16[192,512]{1,0:T(8,128)(2,1)S(1)}, u32[]{:S(2)}, u32[]{:S(2)}) collective-permute-start(bf16[192,512]{1,0:T(8,128)(2,1)} %kg_own.3), channel_id=1, source_target_pairs={{0,1},{1,0},{2,3},{3,2},{4,5},{5,4},{6,7},{7,6},{8,9},{9,8},{10,11... | collective-permute-start | bytes 589832 | tf_op jit(solution)/shard_map/ppermute | solution.py:317
  10.7 6.3 %copy-start.2 = (f32[384,128]{1,0:T(8,128)}, f32[384,128]{1,0:T(8,128)S(1)}, u32[]{:S(2)}) copy-start(f32[384,128]{1,0:T(8,128)S(1)} %get-tuple-element.19.sin) | copy-start | bytes 589828
  10.7 6.3 %copy-start.4 = (f32[384,128]{1,0:T(8,128)}, f32[384,128]{1,0:T(8,128)S(1)}, u32[]{:S(2)}) copy-start(f32[384,128]{1,0:T(8,128)S(1)} %get-tuple-element.20.cos) | copy-start | bytes 589828
  11.2 5.8 %copy-start.10 = (bf16[192,512]{1,0:T(8,128)(2,1)}, bf16[192,512]{1,0:T(8,128)(2,1)S(1)}, u32[]{:S(2)}) copy-start(bf16[192,512]{1,0:T(8,128)(2,1)S(1)} %collective-permute-done.1.kg_other) | copy-start | bytes 589828
  11.2 5.8 %copy-start.1 = (bf16[192,4096]{1,0:T(8,128)(2,1)}, bf16[192,4096]{1,0:T(8,128)(2,1)S(1)}, u32[]{:S(2)}) copy-start(bf16[192,4096]{1,0:T(8,128)(2,1)S(1)} %collective-permute-done.other) | copy-start | bytes 4718596
  11.2 2.0 %copy-start = (bf16[192,4096]{1,0:T(8,128)(2,1)S(1)}, bf16[192,4096]{1,0:T(8,128)(2,1)}, u32[]{:S(2)}) copy-start(bf16[192,4096]{1,0:T(8,128)(2,1)} %own.3) | copy-start | bytes 4718596
  13.2 0.9 copy-start.9
  17.0 18.2 %copy-start.13 = (bf16[2,128,512]{2,1,0:T(8,128)(2,1)}, bf16[2,128,512]{2,1,0:T(8,128)(2,1)S(1)}, u32[]{:S(2)}) copy-start(bf16[2,128,512]{2,1,0:T(8,128)(2,1)S(1)} %get-tuple-element.11.refs_0_) | copy-start | bytes 786436
  17.1 50.0 %all-to-all-start = ((bf16[16,256,256]{2,1,0:T(8,128)(2,1)}), bf16[16,256,256]{2,1,0:T(8,128)(2,1)S(1)}, u32[]{:S(2)}, u32[]{:S(2)}) async-start(bf16[16,256,256]{2,1,0:T(8,128)(2,1)} %bitcast.4), calls=%async_computation | async-start | bytes 4194304 | tf_op jit(solution)/shard_map/all_to_all | solution.py:328
  33.3 11.5 %collective-permute-start.3 = (bf16[2,128,512]{2,1,0:T(8,128)(2,1)S(1)}, bf16[2,128,512]{2,1,0:T(8,128)(2,1)S(1)}, u32[]{:S(2)}, u32[]{:S(2)}) collective-permute-start(bf16[2,128,512]{2,1,0:T(8,128)(2,1)S(1)} %get-tuple-element.11.refs_0_), channel_id=1, source_target_pairs={{0,2},{2,4},{4,6},{6,8},{8,10},{10,12},{12,14},{14,0},{1,3},{3,5},... | collective-permute-start | bytes 786440 | tf_op jit(solution)/shard_map/ppermute | solution.py:74
  35.2 11.4 %collective-permute-start.7 = (bf16[2,128,512]{2,1,0:T(8,128)(2,1)S(1)}, bf16[2,128,512]{2,1,0:T(8,128)(2,1)S(1)}, u32[]{:S(2)}, u32[]{:S(2)}) collective-permute-start(bf16[2,128,512]{2,1,0:T(8,128)(2,1)S(1)} %get-tuple-element.11.refs_0_), channel_id=1, source_target_pairs={{0,14},{2,0},{4,2},{6,4},{8,6},{10,8},{12,10},{14,12},{1,15},{3,1}... | collective-permute-start | bytes 786440 | tf_op jit(solution)/shard_map/ppermute | solution.py:75
  44.7 38.1 %copy-start.16 = (bf16[2,128,512]{2,1,0:T(8,128)(2,1)}, bf16[2,128,512]{2,1,0:T(8,128)(2,1)S(1)}, u32[]{:S(2)}) copy-start(bf16[2,128,512]{2,1,0:T(8,128)(2,1)S(1)} %collective-permute-done.3.refs_1_) | copy-start | bytes 786436
  44.7 10.6 %collective-permute-start.4 = (bf16[2,128,512]{2,1,0:T(8,128)(2,1)S(1)}, bf16[2,128,512]{2,1,0:T(8,128)(2,1)S(1)}, u32[]{:S(2)}, u32[]{:S(2)}) collective-permute-start(bf16[2,128,512]{2,1,0:T(8,128)(2,1)S(1)} %collective-permute-done.3.refs_1_), channel_id=1, source_target_pairs={{0,2},{2,4},{4,6},{6,8},{8,10},{10,12},{12,14},{14,0},{1,3},{3,5},... | collective-permute-start | bytes 786440 | tf_op jit(solution)/shard_map/ppermute | solution.py:74
  46.7 20.4 %copy-start.17 = (bf16[2,128,512]{2,1,0:T(8,128)(2,1)}, bf16[2,128,512]{2,1,0:T(8,128)(2,1)S(1)}, u32[]{:S(2)}) copy-start(bf16[2,128,512]{2,1,0:T(8,128)(2,1)S(1)} %collective-permute-done.7.refs_5_) | copy-start | bytes 786436
  46.7 10.6 %collective-permute-start.8 = (bf16[2,128,512]{2,1,0:T(8,128)(2,1)S(1)}, bf16[2,128,512]{2,1,0:T(8,128)(2,1)S(1)}, u32[]{:S(2)}, u32[]{:S(2)}) collective-permute-start(bf16[2,128,512]{2,1,0:T(8,128)(2,1)S(1)} %collective-permute-done.7.refs_5_), channel_id=1, source_target_pairs={{0,14},{2,0},{4,2},{6,4},{8,6},{10,8},{12,10},{14,12},{1,15},{3,1}... | collective-permute-start | bytes 786440 | tf_op jit(solution)/shard_map/ppermute | solution.py:75
  55.4 11.6 %copy-start.18 = (bf16[2,128,512]{2,1,0:T(8,128)(2,1)}, bf16[2,128,512]{2,1,0:T(8,128)(2,1)S(1)}, u32[]{:S(2)}) copy-start(bf16[2,128,512]{2,1,0:T(8,128)(2,1)S(1)} %collective-permute-done.4.refs_2_) | copy-start | bytes 786436
  55.4 9.7 %collective-permute-start.5 = (bf16[2,128,512]{2,1,0:T(8,128)(2,1)S(1)}, bf16[2,128,512]{2,1,0:T(8,128)(2,1)S(1)}, u32[]{:S(2)}, u32[]{:S(2)}) collective-permute-start(bf16[2,128,512]{2,1,0:T(8,128)(2,1)S(1)} %collective-permute-done.4.refs_2_), channel_id=1, source_target_pairs={{0,2},{2,4},{4,6},{6,8},{8,10},{10,12},{12,14},{14,0},{1,3},{3,5},... | collective-permute-start | bytes 786440 | tf_op jit(solution)/shard_map/ppermute | solution.py:74
  57.3 25.6 %copy-start.19 = (bf16[2,128,512]{2,1,0:T(8,128)(2,1)}, bf16[2,128,512]{2,1,0:T(8,128)(2,1)S(1)}, u32[]{:S(2)}) copy-start(bf16[2,128,512]{2,1,0:T(8,128)(2,1)S(1)} %collective-permute-done.8.refs_6_) | copy-start | bytes 786436
  57.3 9.7 %collective-permute-start.9 = (bf16[2,128,512]{2,1,0:T(8,128)(2,1)S(1)}, bf16[2,128,512]{2,1,0:T(8,128)(2,1)S(1)}, u32[]{:S(2)}, u32[]{:S(2)}) collective-permute-start(bf16[2,128,512]{2,1,0:T(8,128)(2,1)S(1)} %collective-permute-done.8.refs_6_), channel_id=1, source_target_pairs={{0,14},{2,0},{4,2},{6,4},{8,6},{10,8},{12,10},{14,12},{1,15},{3,1}... | collective-permute-start | bytes 786440 | tf_op jit(solution)/shard_map/ppermute | solution.py:75
  65.1 17.8 %copy-start.7 = (bf16[2,128,512]{2,1,0:T(8,128)(2,1)}, bf16[2,128,512]{2,1,0:T(8,128)(2,1)S(1)}, u32[]{:S(2)}) copy-start(bf16[2,128,512]{2,1,0:T(8,128)(2,1)S(1)} %collective-permute-done.5.after_right.refs_3_) | copy-start | bytes 786436
  65.1 17.8 %collective-permute-start.6 = (bf16[2,128,512]{2,1,0:T(8,128)(2,1)S(1)}, bf16[2,128,512]{2,1,0:T(8,128)(2,1)}, u32[]{:S(2)}, u32[]{:S(2)}) collective-permute-start(bf16[2,128,512]{2,1,0:T(8,128)(2,1)S(1)} %collective-permute-done.5.after_right.refs_3_), channel_id=1, source_target_pairs={{0,2},{2,4},{4,6},{6,8},{8,10},{10,12},{12,14},{14,0},{1,3},{3,5},... | collective-permute-start | bytes 786440 | tf_op jit(solution)/shard_map/ppermute | solution.py:76
  67.0 15.9 %copy-start.8 = (bf16[2,128,512]{2,1,0:T(8,128)(2,1)}, bf16[2,128,512]{2,1,0:T(8,128)(2,1)S(1)}, u32[]{:S(2)}) copy-start(bf16[2,128,512]{2,1,0:T(8,128)(2,1)S(1)} %collective-permute-done.9.after_left.refs_7_) | copy-start | bytes 786436
  67.3 15.6 %copy-start.6 = (bf16[256,512]{1,0:T(8,128)(2,1)}, bf16[256,512]{1,0:T(8,128)(2,1)S(1)}, u32[]{:S(2)}) copy-start(bf16[256,512]{1,0:T(8,128)(2,1)S(1)} %near_total.1.refs_8_) | copy-start | bytes 786436
  68.2 36.2 %all-to-all-start.1 = ((bf16[64,4,512]{2,1,0:T(4,128)(2,1)}), bf16[64,4,512]{2,1,0:T(4,128)(2,1)S(1)}, u32[]{:S(2)}, u32[]{:S(2)}) async-start(bf16[64,4,512]{2,1,0:T(4,128)(2,1)} %all_to_all.10), calls=%async_computation.1 | async-start | bytes 524288 | tf_op jit(solution)/shard_map/all_to_all | solution.py:330
  82.9 13.4 %copy-start.3 = (f32[384,128]{1,0:T(8,128)S(1)}, f32[384,128]{1,0:T(8,128)}, u32[]{:S(2)}) copy-start(f32[384,128]{1,0:T(8,128)} %copy-done.2) | copy-start | bytes 589828
  82.9 13.4 %copy-start.5 = (f32[384,128]{1,0:T(8,128)S(1)}, f32[384,128]{1,0:T(8,128)}, u32[]{:S(2)}) copy-start(f32[384,128]{1,0:T(8,128)} %copy-done.4) | copy-start | bytes 589828
  90.4 5.9 %collective-permute-start.11 = (bf16[192,2048]{1,0:T(8,128)(2,1)}, bf16[192,2048]{1,0:T(8,128)(2,1)S(1)}, u32[]{:S(2)}, u32[]{:S(2)}) collective-permute-start(bf16[192,2048]{1,0:T(8,128)(2,1)} %get-tuple-element.16), channel_id=1, source_target_pairs={{0,1},{1,0},{2,3},{3,2},{4,5},{5,4},{6,7},{7,6},{8,9},{9,8},{10,11... | collective-permute-start | bytes 2359304 | tf_op jit(solution)/shard_map/ppermute | solution.py:339
  92.4 4.0 %collective-permute-start.10 = (f32[192,512]{1,0:T(8,128)}, f32[192,512]{1,0:T(8,128)S(1)}, u32[]{:S(2)}, u32[]{:S(2)}) collective-permute-start(f32[192,512]{1,0:T(8,128)} %get-tuple-element.15), channel_id=1, source_target_pairs={{0,1},{1,0},{2,3},{3,2},{4,5},{5,4},{6,7},{7,6},{8,9},{9,8},{10,11... | collective-permute-start | bytes 1179656 | tf_op jit(solution)/shard_map/ppermute | solution.py:338
  96.3 1.1 %copy-start.11 = (bf16[192,2048]{1,0:T(8,128)(2,1)S(1)}, bf16[192,2048]{1,0:T(8,128)(2,1)}, u32[]{:S(2)}) copy-start(bf16[192,2048]{1,0:T(8,128)(2,1)} %get-tuple-element.14.t_own) | copy-start | bytes 2359300
  97.5 1.0 copy-start.12
  (2 other events, 1.6 us)
